TPU v7x, 32 devices: a whole 2x2x4 slice. The times are simulated.
32 devices in a mesh: dp: 4 (over z), context: 4 (over y, x), tensor: 2 (over core).
Axes of the slice: x: 2, y: 2, z: 4, core: 2. Of those that a mesh axis runs over, the one named last changes fastest.
Arguments:
- inputs: bfloat16 [8192, 5376], P(('dp', 'context')), may hold values from -8 to 8
- queries: bfloat16 [8192, 2048], P(('dp', 'context'), 'tensor'), may hold values from -8 to 8
- key_states: bfloat16 [8192, 1024], P(('dp', 'context'), 'tensor'), may hold values from -8 to 8
- value_states: bfloat16 [8192, 1024], P(('dp', 'context'), 'tensor'), may hold values from -6 to 6
- out_grad: bfloat16 [8192, 5376], P(('dp', 'context')), may hold values from -8 to 8
- positions: int32 [8192], P(('dp', 'context')), may hold values from 0 to 10239, as said below
- w_query: bfloat16 [5376, 2048], P(None, 'tensor'), may hold values from -0.078125 to 0.078125
- w_key: bfloat16 [5376, 1024], P(None, 'tensor'), may hold values from -0.078125 to 0.078125
- w_value: bfloat16 [5376, 1024], P(None, 'tensor'), may hold values from -0.078125 to 0.078125
- w_output: bfloat16 [5376, 2048], P(None, 'tensor'), may hold values from -0.125 to 0.125
Outputs:
- input_grad: bfloat16 [8192, 5376], P(('dp', 'context', 'tensor'))
- grad_query: float32 [5376, 2048], P(('dp', 'context'), 'tensor')
- grad_key: float32 [5376, 1024], P(('dp', 'context'), 'tensor')
- grad_value: float32 [5376, 1024], P(('dp', 'context'), 'tensor')
- grad_output: float32 [5376, 2048], P(('dp', 'context'), 'tensor')
Inputs may be any that keep to these rules, and one draw needn't show every extreme that they name: Within a document positions rise by one from token to token; a position of 0 starts a new document; the first document of each replica's 2048 tokens may have begun before them.
All inputs are finite; a program needn't handle non-finite values.
Results may differ from a plain program's by a relative error of at most 0.02.
Values may be sent and summed in bfloat16 or wider, within the bound.
No kernel may reach another device: no remote copies, remote signals or barrier semaphores. Data moves between devices by JAX's collectives and lax.ppermute only.
A program may use at most 192 MiB of HBM per device.

v0:
```python
import functools

import jax
import jax.numpy as jnp
from jax import lax
from jax.experimental import pallas as pl
from jax.experimental.pallas import tpu as pltpu
from jax.sharding import PartitionSpec as P

HD = 128
W = 1024
QSCALAR = 168


def shifted(x, axis, by):
    count = lax.axis_size(axis)
    pairs = [(i, i + by) for i in range(count) if 0 <= i + by < count]
    return lax.ppermute(x, axis, pairs)


def rotate_back(grads, places):
    count = grads.shape[0]
    half = HD // 2
    index = jnp.arange(half, dtype=jnp.float32)
    freq = jnp.power(jnp.float32(10000.0), index * (-2.0 / HD))
    angle = places.astype(jnp.float32)[:, None] * freq[None, :]
    cosine = jnp.cos(angle)[:, None, :]
    sine = jnp.sin(angle)[:, None, :]
    split = grads.reshape(count, -1, 2, half)
    first = split[:, :, 0, :]
    second = split[:, :, 1, :]
    upper = first * cosine + second * sine
    lower = second * cosine - first * sine
    return jnp.stack([upper, lower], axis=2).reshape(count, -1)


def contract_rows(left, right):
    return lax.dot_general(
        left, right, (((0,), (0,)), ((), ())), preferred_element_type=jnp.float32
    )


def contract_cols(left, right):
    return lax.dot_general(
        left, right, (((1,), (1,)), ((), ())), preferred_element_type=jnp.float32
    )


def banded(
    inputs,
    queries,
    key_states,
    value_states,
    out_grad,
    positions,
    w_query,
    w_key,
    w_value,
    w_output,
):
    count = queries.shape[0]
    head_cols = queries.shape[1]
    kv_cols = key_states.shape[1]
    kv_here = kv_cols // HD
    group = head_cols // kv_cols
    scale = QSCALAR ** (-0.5)
    block = lax.axis_index("context")
    blocks = lax.axis_size("context")
    reach = min((W + count - 2) // count, blocks - 1)
    span = (reach + 1) * count
    key_pieces = []
    value_pieces = []
    for back in range(reach, 0, -1):
        earlier_keys, earlier_values = shifted((key_states, value_states), "context", back)
        key_pieces.append(earlier_keys)
        value_pieces.append(earlier_values)
    band_keys = jnp.concatenate(key_pieces + [key_states], axis=0)
    band_values = jnp.concatenate(value_pieces + [value_states], axis=0)
    query_index = block * count + jnp.arange(count, dtype=jnp.int32)
    key_index = (block - reach) * count + jnp.arange(span, dtype=jnp.int32)
    doc_start = query_index - positions
    allowed = (key_index[None, :] <= query_index[:, None]) & (
        query_index[:, None] - key_index[None, :] < W
    )
    allowed = allowed & (key_index[None, :] >= doc_start[:, None]) & (key_index[None, :] >= 0)
    query_heads = queries.reshape(count, kv_here, group, HD)
    key_heads = band_keys.reshape(span, kv_here, HD)
    value_heads = band_values.reshape(span, kv_here, HD)
    scores = (
        jnp.einsum("qhgd,khd->hgqk", query_heads, key_heads, preferred_element_type=jnp.float32)
        * scale
    )
    scores = jnp.where(allowed, scores, -1e30)
    top = jnp.max(scores, axis=-1, keepdims=True)
    weights = jnp.exp(scores - top)
    probs = weights / jnp.sum(weights, axis=-1, keepdims=True)
    probs_half = probs.astype(jnp.bfloat16)
    attn = jnp.einsum(
        "hgqk,khd->qhgd", probs_half, value_heads, preferred_element_type=jnp.float32
    ).astype(jnp.bfloat16)
    attn_flat = attn.reshape(count, head_cols)
    dattn = jnp.dot(out_grad, w_output, preferred_element_type=jnp.float32).astype(jnp.bfloat16)
    dattn_heads = dattn.reshape(count, kv_here, group, HD)
    dprobs = jnp.einsum(
        "qhgd,khd->hgqk", dattn_heads, value_heads, preferred_element_type=jnp.float32
    )
    delta = jnp.sum(dattn_heads.astype(jnp.float32) * attn.astype(jnp.float32), axis=-1)
    delta = jnp.transpose(delta, (1, 2, 0))[..., None]
    dscores = (probs * (dprobs - delta) * scale).astype(jnp.bfloat16)
    query_grad = jnp.einsum(
        "hgqk,khd->qhgd", dscores, key_heads, preferred_element_type=jnp.float32
    ).reshape(count, head_cols)
    band_key_grad = jnp.einsum(
        "hgqk,qhgd->khd", dscores, query_heads, preferred_element_type=jnp.float32
    ).reshape(span, kv_cols)
    band_value_grad = jnp.einsum(
        "hgqk,qhgd->khd", probs_half, dattn_heads, preferred_element_type=jnp.float32
    ).reshape(span, kv_cols)
    key_grad = band_key_grad[reach * count :]
    value_grad = band_value_grad[reach * count :]
    for back in range(1, reach + 1):
        first_row = (reach - back) * count
        sent_keys, sent_values = shifted(
            (
                band_key_grad[first_row : first_row + count],
                band_value_grad[first_row : first_row + count],
            ),
            "context",
            -back,
        )
        key_grad = key_grad + sent_keys
        value_grad = value_grad + sent_values
    query_lin = rotate_back(query_grad, positions).astype(jnp.bfloat16)
    key_lin = rotate_back(key_grad, positions).astype(jnp.bfloat16)
    value_half = value_grad.astype(jnp.bfloat16)
    total = contract_cols(query_lin, w_query)
    total = total + contract_cols(key_lin, w_key)
    total = total + contract_cols(value_half, w_value)
    input_grad = lax.psum_scatter(total, "tensor", scatter_dimension=0, tiled=True).astype(
        jnp.bfloat16
    )
    terms = (
        contract_rows(inputs, query_lin),
        contract_rows(inputs, key_lin),
        contract_rows(inputs, value_half),
        contract_rows(out_grad, attn_flat),
    )
    summed = (
        lax.psum_scatter(
            terms[0].astype(jnp.bfloat16), ("dp", "context"), scatter_dimension=0, tiled=True
        ).astype(jnp.float32),
        lax.psum_scatter(
            terms[1].astype(jnp.bfloat16), ("dp", "context"), scatter_dimension=0, tiled=True
        ).astype(jnp.float32),
        lax.psum_scatter(
            terms[2].astype(jnp.bfloat16), ("dp", "context"), scatter_dimension=0, tiled=True
        ).astype(jnp.float32),
        lax.psum_scatter(
            terms[3].astype(jnp.bfloat16), ("dp", "context"), scatter_dimension=0, tiled=True
        ).astype(jnp.float32),
    )
    return (input_grad, summed[0], summed[1], summed[2], summed[3])


TILE = 256
EXTRA = 16
RADIX = 128
NEGATIVE = -1e30
LOG2E = 1.4426950408889634
VMEM_LIMIT = 48 * 1024 * 1024
LOAD = 40
LOAD1 = 12
LOAD2 = 12
COST = 80
VMEM_MOST = 60 * 1024 * 1024


def dot_nt(left, right):
    return lax.dot_general(
        left, right, (((1,), (1,)), ((), ())), preferred_element_type=jnp.float32
    )


def dot_nn(left, right):
    return lax.dot_general(
        left, right, (((1,), (0,)), ((), ())), preferred_element_type=jnp.float32
    )


def whole():
    return pl.BlockSpec(memory_space=pltpu.VMEM)


def scalars():
    return pl.BlockSpec(memory_space=pltpu.SMEM)


def params(limit=VMEM_LIMIT):
    return pltpu.CompilerParams(vmem_limit_bytes=limit)


def aligned(index, size):
    return pl.ds(pl.multiple_of(index * size, size), size)


def pack_heads_kernel(blocks, wide, narrow, at_ref, q_ref, k_ref, v_ref, extra_ref, *outs):
    me = at_ref[0]
    count = q_ref.shape[0]
    for part in range(blocks):
        there = me ^ part
        out = outs[part]
        out[:count, :wide] = q_ref[:, aligned(there, wide)]
        out[:count, wide : wide + narrow] = k_ref[:, aligned(there, narrow)]
        out[:count, wide + narrow :] = v_ref[:, aligned(there, narrow)]
        out[count:, :] = extra_ref[...]


def pack_heads(at, queries, key_states, value_states, extra, blocks, wide, narrow):
    count = queries.shape[0]
    shape = jax.ShapeDtypeStruct((count + EXTRA, wide + 2 * narrow), queries.dtype)
    return pl.pallas_call(
        functools.partial(pack_heads_kernel, blocks, wide, narrow),
        out_shape=(shape,) * blocks,
        in_specs=[scalars()] + [whole()] * 4,
        out_specs=(whole(),) * blocks,
        compiler_params=params(),
        cost_estimate=pl.CostEstimate(
            flops=0, bytes_accessed=4 * blocks * count * (wide + 2 * narrow), transcendentals=0
        ),
        name="pack_heads",
    )(at, queries, key_states, value_states, extra)


def pack_rows_kernel(blocks, replicas, rows, at_ref, x_ref, own_ref, *rest):
    outs, turned = rest[:-1], rest[-1]
    me, side = at_ref[0], at_ref[1]
    count, width = x_ref.shape
    half = count // 2

    def turn(index, carry):
        cols = aligned(index, HD)
        turned[cols, :] = x_ref[:, cols].T
        return carry

    lax.fori_loop(0, width // HD, turn, 0)
    for replica in range(replicas):
        into = pl.ds(replica * rows, rows)
        own_ref[into, :] = turned[aligned(replica * blocks + me, rows), :]
        for part in range(1, blocks):
            taken = aligned(replica * blocks + (me ^ part), rows)
            outs[part - 1][into, :] = turned[taken, aligned(side, half)]


def pack_rows(at, x, blocks, replicas):
    count, width = x.shape
    rows = width // (replicas * blocks)
    share = replicas * rows
    own = jax.ShapeDtypeStruct((share, count), x.dtype)
    sent = jax.ShapeDtypeStruct((share, count // 2), x.dtype)
    return pl.pallas_call(
        functools.partial(pack_rows_kernel, blocks, replicas, rows),
        out_shape=(own,) + (sent,) * (blocks - 1),
        in_specs=[scalars(), whole()],
        out_specs=(whole(),) * blocks,
        scratch_shapes=[pltpu.VMEM((width, count), x.dtype)],
        compiler_params=params(),
        cost_estimate=pl.CostEstimate(
            flops=0, bytes_accessed=6 * count * width, transcendentals=0
        ),
        name="pack_rows",
    )(at, x)


def attention_kernel(blocks, count, heads, group, *refs):
    at_ref = refs[0]
    packs = refs[1 : 1 + blocks]
    dpacks = refs[1 + blocks : 1 + 2 * blocks]
    low_ref, cos_ref, sin_ref = refs[1 + 2 * blocks : 4 + 2 * blocks]
    first_ref, second_ref = refs[4 + 2 * blocks : 6 + 2 * blocks]
    q_s, k_s, v_s, kt_s, vt_s, d_s, dt_s, dk_s, dv_s = refs[6 + 2 * blocks :]
    scale = QSCALAR ** (-0.5)
    factor = scale * LOG2E
    span = blocks * count
    wide = heads * group * HD
    narrow = heads * HD
    per_block = count // TILE
    reach = -(-(W - 1) // TILE)
    me = at_ref[0]
    for part in range(blocks):
        rows = aligned(me ^ part, count)
        pack = packs[part]
        q_s[rows, :] = pack[:count, :wide]
        keys = pack[:count, wide : wide + narrow]
        values = pack[:count, wide + narrow :]
        k_s[rows, :] = keys
        v_s[rows, :] = values
        kt_s[:, rows] = keys.T
        vt_s[:, rows] = values.T
        d_s[rows, :] = dpacks[part][...]
        dt_s[:, rows] = dpacks[part][...].T
    dk_s[...] = jnp.zeros_like(dk_s)
    dv_s[...] = jnp.zeros_like(dv_s)

    def stored(index):
        return aligned(((index // per_block) ^ me) * per_block + lax.rem(index, per_block), TILE)

    def rotated(grad, rows):
        return grad * cos_ref[rows, :] + pltpu.roll(grad, HD // 2, 1) * sin_ref[rows, :]

    for head in range(heads):
        kv = slice(head * HD, (head + 1) * HD)

        def tile(index, first_key, width):
            index = jnp.int32(index)
            q_rows = aligned(index, TILE)
            t_rows = stored(index)
            k_rows = pl.ds(first_key, width)
            columns = [slice(head * group * HD + g * HD, head * group * HD + (g + 1) * HD) for g in range(group)]
            query = jnp.concatenate([q_s[q_rows, c] for c in columns], axis=0)
            dattn = jnp.concatenate([d_s[q_rows, c] for c in columns], axis=0)
            dattn_t = jnp.concatenate([dt_s[c, q_rows] for c in columns], axis=1)
            scores = dot_nt(k_s[k_rows, kv], query)
            low = jnp.concatenate([low_ref[:, t_rows]] * group, axis=1)
            at = first_key + lax.broadcasted_iota(jnp.int32, (width, group * TILE), 0)
            own = index * TILE + lax.rem(
                lax.broadcasted_iota(jnp.int32, (1, group * TILE), 1), jnp.int32(TILE)
            )
            scores = jnp.where((at >= low) & (at <= own), scores, NEGATIVE)
            top = jnp.max(scores, axis=0, keepdims=True)
            weights = jnp.exp2(scores * factor - top * factor)
            inverse = 1.0 / jnp.sum(weights, axis=0, keepdims=True)
            probs = weights * inverse
            half = probs.astype(jnp.bfloat16)
            attn = dot_nn(vt_s[kv, k_rows], half).astype(jnp.bfloat16)
            dprobs = dot_nt(v_s[k_rows, kv], dattn)
            attn_wide = attn.astype(jnp.float32)
            delta = jnp.sum(dattn_t.astype(jnp.float32) * attn_wide, axis=0, keepdims=True)
            dscores = (probs * (dprobs - delta)).astype(jnp.bfloat16)
            query_grad = (dot_nn(kt_s[kv, k_rows], dscores) * scale).T
            attn_rows = attn_wide.T
            dk_s[k_rows, kv] += dot_nn(dscores, query)
            dv_s[k_rows, kv] += dot_nn(half, dattn)
            for g, c in enumerate(columns):
                part = slice(g * TILE, (g + 1) * TILE)
                first_ref[q_rows, c] = attn_rows[part].astype(jnp.bfloat16)
                second_ref[q_rows, c] = rotated(query_grad[part], t_rows).astype(jnp.bfloat16)

        tiles = span // TILE
        for index in range(min(reach, tiles)):
            tile(index, 0, (index + 1) * TILE)

        def steady(index, carry):
            tile(index, pl.multiple_of((index - reach) * TILE, TILE), (reach + 1) * TILE)
            return carry

        if tiles > reach:
            lax.fori_loop(reach, tiles, steady, 0)
        out = slice(wide + head * HD, wide + (head + 1) * HD)
        for index in range(tiles):
            rows = pl.ds(index * TILE, TILE)
            first_ref[rows, out] = dv_s[rows, kv].astype(jnp.bfloat16)
            second_ref[rows, out] = rotated(
                dk_s[rows, kv] * scale, stored(jnp.int32(index))
            ).astype(jnp.bfloat16)


def attention(at, packs, dpacks, low, cosine, sine, heads, group):
    blocks = len(packs)
    count = dpacks[0].shape[0]
    span = blocks * count
    wide = heads * group * HD
    narrow = heads * HD
    half = jnp.bfloat16
    pairs = heads * group * span * (W + TILE)
    return pl.pallas_call(
        functools.partial(attention_kernel, blocks, count, heads, group),
        out_shape=(jax.ShapeDtypeStruct((span, wide + narrow), half),) * 2,
        in_specs=[scalars()] + [whole()] * (2 * blocks + 3),
        out_specs=(whole(),) * 2,
        scratch_shapes=[
            pltpu.VMEM((span, wide), half),
            pltpu.VMEM((span, narrow), half),
            pltpu.VMEM((span, narrow), half),
            pltpu.VMEM((narrow, span), half),
            pltpu.VMEM((narrow, span), half),
            pltpu.VMEM((span, wide), half),
            pltpu.VMEM((wide, span), half),
            pltpu.VMEM((span, narrow), jnp.float32),
            pltpu.VMEM((span, narrow), jnp.float32),
        ],
        compiler_params=params(),
        cost_estimate=pl.CostEstimate(
            flops=10 * pairs * HD, bytes_accessed=span * wide * 12, transcendentals=pairs
        ),
        name="attention_backward",
    )(at, *packs, *dpacks, low, cosine, sine)


def weight_terms_kernel(blocks, jobs, at_ref, *refs):
    pieces = 1 + 2 * (blocks - 1)
    sets = 1 + max(job[0] for job in jobs)
    piece_refs = refs[: sets * pieces]
    lin_refs = refs[sets * pieces : -1]
    out_ref = refs[-1]
    me, side = at_ref[0], at_ref[1]
    count = piece_refs[0].shape[1]
    half = count // 2
    rows = [aligned(me, count)]
    for part in range(1, blocks):
        rows.append(aligned((me ^ part) * 2 + side, half))
        rows.append(aligned((me ^ part) * 2 + 1 - side, half))
    total = [None] * len(jobs)
    for piece in range(pieces):
        for index, (which, lin, low, high) in enumerate(jobs):
            left = piece_refs[which * pieces + piece][...]
            term = dot_nn(left, lin_refs[lin][rows[piece], low:high])
            total[index] = term if total[index] is None else total[index] + term
    first = 0
    for index, (which, lin, low, high) in enumerate(jobs):
        out_ref[:, first : first + high - low] = total[index].astype(out_ref.dtype)
        first += high - low


def weight_terms(at, sets, lins, jobs, blocks, replicas, load=LOAD):
    share = sets[0][0].shape[0]
    rows = share // replicas
    span = lins[0].shape[0]
    cols = sum(job[3] - job[2] for job in jobs)
    pieces = [x for one in sets for x in one]

    def piece(x):
        return pl.BlockSpec((rows, x.shape[1]), lambda i, at: (i, 0))

    def fixed(x):
        return pl.BlockSpec(x.shape, lambda i, at: (0, 0))

    return pl.pallas_call(
        functools.partial(weight_terms_kernel, blocks, jobs),
        out_shape=jax.ShapeDtypeStruct((share, cols), lins[0].dtype),
        grid_spec=pltpu.PrefetchScalarGridSpec(
            num_scalar_prefetch=1,
            grid=(replicas,),
            in_specs=[piece(x) for x in pieces] + [fixed(x) for x in lins],
            out_specs=pl.BlockSpec((rows, cols), lambda i, at: (i, 0)),
        ),
        compiler_params=params(VMEM_MOST),
        cost_estimate=pl.CostEstimate(
            flops=load * share * span * cols,
            bytes_accessed=2 * share * span * len(sets) + 2 * (span + share) * cols,
            transcendentals=0,
        ),
        name="weight_terms",
    )(at, *pieces, *lins)


def assemble_kernel(places, at_ref, *refs):
    parts, outs = refs[:-4], refs[-4:]
    me = at_ref[0]
    for part, one in zip(parts, places):
        first = 0
        for out, source, cols in one:
            outs[out][:, aligned(me ^ source, cols)] = part[:, first : first + cols].astype(
                jnp.float32
            )
            first += cols


def assemble(at, places, parts, blocks, wide, narrow):
    rows = parts[0].shape[0]
    shapes = [
        jax.ShapeDtypeStruct((rows, blocks * cols), jnp.float32)
        for cols in (wide, narrow, wide, narrow)
    ]
    return pl.pallas_call(
        functools.partial(assemble_kernel, places),
        out_shape=tuple(shapes),
        in_specs=[scalars()] + [whole()] * len(parts),
        out_specs=(whole(),) * 4,
        compiler_params=params(),
        name="assemble",
    )(at, *parts)


def input_first_kernel(blocks, wide, narrow, at_ref, *refs):
    firsts, seconds = refs[: blocks - 1], refs[blocks - 1 : 2 * (blocks - 1)]
    wq_ref, wk_ref, wv_ref, out_ref, q_s, k_s, v_s = refs[2 * (blocks - 1) :]
    me = at_ref[0]

    @pl.when(pl.program_id(0) == 0)
    def _():
        q_s[...] = jnp.zeros_like(q_s)
        k_s[...] = jnp.zeros_like(k_s)
        v_s[...] = jnp.zeros_like(v_s)
        for part in range(blocks - 1):
            there = me ^ part
            q_s[:, aligned(there, wide)] = seconds[part][:, :wide]
            k_s[:, aligned(there, narrow)] = seconds[part][:, wide:]
            v_s[:, aligned(there, narrow)] = firsts[part][:, wide:]

    total = dot_nt(q_s[...], wq_ref[...])
    total = total + dot_nt(k_s[...], wk_ref[...])
    out_ref[...] = total + dot_nt(v_s[...], wv_ref[...])


def input_last_kernel(wide, at_ref, first_ref, second_ref, wq_ref, wk_ref, wv_ref, part_ref, mine_ref, sent_ref, total_s):
    side = at_ref[1]
    half = first_ref.shape[0] // 2
    total = part_ref[...] + dot_nt(second_ref[:, :wide], wq_ref[...])
    total = total + dot_nt(second_ref[:, wide:], wk_ref[...])
    total_s[...] = total + dot_nt(first_ref[:, wide:], wv_ref[...])
    for target, which in ((sent_ref, 1 - side), (mine_ref, side)):
        target[...] = total_s[aligned(which, half), :].astype(target.dtype)


def columns_step(width):
    return next(s for s in (768, 512, 256, 128, width) if width % s == 0)


def input_first(at, firsts, seconds, w_query, w_key, w_value, count, wide, narrow):
    blocks = len(firsts) + 1
    width = w_query.shape[0]
    step = columns_step(width)
    ins = firsts + seconds
    half = jnp.bfloat16
    return pl.pallas_call(
        functools.partial(input_first_kernel, blocks, wide, narrow),
        out_shape=jax.ShapeDtypeStruct((count, width), jnp.float32),
        grid_spec=pltpu.PrefetchScalarGridSpec(
            num_scalar_prefetch=1,
            grid=(width // step,),
            in_specs=[pl.BlockSpec((count, x.shape[1]), lambda i, at: (at[0], 0)) for x in ins]
            + [
                pl.BlockSpec((step, x.shape[1]), lambda i, at: (i, 0))
                for x in (w_query, w_key, w_value)
            ],
            out_specs=pl.BlockSpec((count, step), lambda i, at: (0, i)),
            scratch_shapes=[
                pltpu.VMEM((count, blocks * wide), half),
                pltpu.VMEM((count, blocks * narrow), half),
                pltpu.VMEM((count, blocks * narrow), half),
            ],
        ),
        compiler_params=params(VMEM_MOST),
        cost_estimate=pl.CostEstimate(
            flops=count * width * blocks * (wide + 2 * narrow), bytes_accessed=0, transcendentals=0
        ),
        name="input_first",
    )(at, *ins, w_query, w_key, w_value)


def input_last(at, far, first, second, partial, w_query, w_key, w_value, wide, narrow):
    count, width = partial.shape
    step = columns_step(width)

    def own(x):
        return pl.BlockSpec((count, x.shape[1]), lambda i, at: (at[0], 0))

    def weight(cols):
        return pl.BlockSpec((step, cols), lambda i, at: (i, at[0] ^ far))

    out = pl.BlockSpec((count // 2, step), lambda i, at: (0, i))
    return pl.pallas_call(
        functools.partial(input_last_kernel, wide),
        out_shape=(
            jax.ShapeDtypeStruct((count // 2, width), jnp.float32),
            jax.ShapeDtypeStruct((count // 2, width), jnp.bfloat16),
        ),
        grid_spec=pltpu.PrefetchScalarGridSpec(
            num_scalar_prefetch=1,
            grid=(width // step,),
            in_specs=[own(first), own(second), weight(wide), weight(narrow), weight(narrow)]
            + [pl.BlockSpec((count, step), lambda i, at: (0, i))],
            out_specs=(out, out),
            scratch_shapes=[pltpu.VMEM((count, step), jnp.float32)],
        ),
        compiler_params=params(VMEM_MOST),
        cost_estimate=pl.CostEstimate(
            flops=COST * count * width * (wide + 2 * narrow), bytes_accessed=0, transcendentals=0
        ),
        name="input_last",
    )(at, first, second, w_query, w_key, w_value, partial)


def swap(x, axis, by):
    count = lax.axis_size(axis)
    return lax.ppermute(x, axis, [(i, i ^ by) for i in range(count)])


def rotation_tables(places):
    half = HD // 2
    index = jnp.arange(half, dtype=jnp.float32)
    freq = jnp.power(jnp.float32(10000.0), index * (-2.0 / HD))
    angle = places.astype(jnp.float32)[:, None] * freq[None, :]
    cosine = jnp.cos(angle)
    sine = jnp.sin(angle)
    return jnp.concatenate([cosine, cosine], axis=1), jnp.concatenate([sine, -sine], axis=1)


def on_device(
    inputs,
    queries,
    key_states,
    value_states,
    out_grad,
    positions,
    w_query,
    w_key,
    w_value,
    w_output,
):
    count = queries.shape[0]
    head_cols = queries.shape[1]
    kv_cols = key_states.shape[1]
    kv_here = kv_cols // HD
    group = head_cols // kv_cols
    blocks = lax.axis_size("context")
    replicas = lax.axis_size("dp")
    cores = lax.axis_size("tensor")
    width = inputs.shape[1]
    heads = kv_here // blocks
    wide = heads * group * HD
    narrow = heads * HD
    fits = (
        blocks == 4
        and kv_here % blocks == 0
        and cores == 2
        and count % (2 * HD) == 0
        and count % TILE == 0
        and W % TILE == 0
        and width % HD == 0
        and width % (replicas * blocks * EXTRA) == 0
        and wide + 2 * narrow >= count
    )
    if not fits:
        return banded(
            inputs, queries, key_states, value_states, out_grad, positions,
            w_query, w_key, w_value, w_output,
        )
    me = lax.axis_index("context")
    side = lax.axis_index("tensor")
    at = jnp.stack([me, side]).astype(jnp.int32)

    barrier = lax.optimization_barrier

    digits = jnp.stack([positions // RADIX, positions % RADIX]).astype(jnp.bfloat16)
    extra = jnp.pad(digits, ((0, EXTRA - 2), (0, wide + 2 * narrow - count)))
    packs = list(
        pack_heads(at, queries, key_states, value_states, extra, blocks, wide, narrow)
    )
    after, packs = barrier((out_grad, packs))
    for part in range(1, blocks):
        packs[part] = swap(packs[part], "context", part)
    dattn = jnp.dot(after, w_output, preferred_element_type=jnp.float32).astype(jnp.bfloat16)
    dpacks = [
        lax.dynamic_slice(dattn, (0, (me ^ part) * wide), (count, wide)) for part in range(blocks)
    ]
    def spread(packed):
        return [swap(x, "context", part + 1) for part, x in enumerate(packed)]

    def joined(own, came):
        pieces = [own]
        for x in came:
            pieces += [x, swap(x, "tensor", 1)]
        return pieces

    soon, dpacks = barrier((at, dpacks))
    packs, dpacks = barrier((packs, dpacks))
    grad_own, *grad_packed = pack_rows(soon, out_grad, blocks, replicas)
    dpacks = [dpacks[0]] + spread(dpacks[1:])
    places = [
        (pack[count, :count].astype(jnp.float32) * RADIX + pack[count + 1, :count].astype(jnp.float32)).astype(jnp.int32)
        for pack in packs[1:]
    ]
    places = jnp.concatenate([positions] + places)
    index = jnp.concatenate(
        [(me ^ part) * count + jnp.arange(count, dtype=jnp.int32) for part in range(blocks)]
    )
    low = jnp.maximum(index - places, index - (W - 1))[None, :]
    cosine, sine = rotation_tables(places)
    soon, grad_packed, packs = barrier((soon, grad_packed, packs))
    input_own, *input_packed = pack_rows(soon, inputs, blocks, replicas)
    dpacks, grad_packed, input_packed = barrier((dpacks, grad_packed, input_packed))

    grad_came = spread(grad_packed)
    first, second = attention(at, packs, dpacks, low, cosine, sine, heads, group)
    first, second, grad_came, input_packed = barrier((first, second, grad_came, input_packed))

    input_came = spread(input_packed)
    grads = joined(grad_own, grad_came)
    edge = wide + narrow
    def summed(term):
        return lax.psum_scatter(term, "dp", scatter_dimension=0, tiled=True)

    parts = []
    term = weight_terms(at, [grads], [first], [(0, 0, 0, wide)], blocks, replicas, LOAD1)
    parts.append(summed(term))
    term, input_came, first, second = barrier((term, input_came, first, second))

    firsts = [first, swap(first, "context", 1), None, None]
    seconds = [second, None, swap(second, "context", 2), None]
    ins = joined(input_own, input_came)
    ins, parts[0] = barrier((ins, parts[0]))
    jobs = [(0, 0, wide, edge), (0, 1, 0, edge)]
    term = weight_terms(at, [ins], [first, second], jobs, blocks, replicas, LOAD2)
    parts.append(summed(term))
    term, firsts[1], seconds[2], first, second = barrier(
        (term, firsts[1], seconds[2], first, second)
    )
    seconds[1] = swap(second, "context", 1)
    firsts[2] = swap(first, "context", 2)
    jobs = [(0, 0, 0, wide), (1, 0, wide, edge), (1, 1, 0, edge)]

    def terms_of(source_first, source_second):
        lins = [firsts[source_first], seconds[source_second]]
        return weight_terms(at, [grads, ins], lins, jobs, blocks, replicas)

    term = terms_of(1, 2)
    parts.append(summed(term))
    term, firsts[1], firsts[2], seconds[1], seconds[2] = barrier(
        (term, firsts[1], firsts[2], seconds[1], seconds[2])
    )
    firsts[3] = swap(firsts[1], "context", 2)
    seconds[3] = swap(seconds[2], "context", 1)
    term = terms_of(2, 1)
    parts.append(summed(term))
    late, term = barrier((at, term))
    partial = input_first(
        late, firsts[:3], seconds[:3], w_query, w_key, w_value, count, wide, narrow
    )
    term, partial, parts[1], firsts[3], seconds[3] = barrier(
        (term, partial, parts[1], firsts[3], seconds[3])
    )
    mine, sent = input_last(
        at, 3, firsts[3], seconds[3], partial, w_query, w_key, w_value, wide, narrow
    )
    came = swap(sent, "tensor", 1)
    mine, firsts[3] = barrier((mine, firsts[3]))
    term = terms_of(3, 3)
    parts.append(summed(term))
    mine, came, parts[2], parts[3] = barrier((mine, came, parts[2], parts[3]))
    input_grad = (mine + came.astype(jnp.float32)).astype(jnp.bfloat16)
    last, input_grad = barrier((at, input_grad))

    def rest(source_first, source_second):
        return [(1, source_first, narrow), (2, source_second, wide), (3, source_second, narrow)]

    layout = [[(0, 0, wide)], rest(0, 0)]
    for source_first, source_second in ((1, 2), (2, 1), (3, 3)):
        layout.append([(0, source_first, wide)] + rest(source_first, source_second))
    grad_output, grad_value, grad_query, grad_key = assemble(
        last, layout, parts, blocks, wide, narrow
    )
    return (input_grad, grad_query, grad_key, grad_value, grad_output)


def solution(mesh):
    return jax.shard_map(
        on_device,
        mesh=mesh,
        in_specs=(
            P(("dp", "context"), None),
            P(("dp", "context"), "tensor"),
            P(("dp", "context"), "tensor"),
            P(("dp", "context"), "tensor"),
            P(("dp", "context"), None),
            P(("dp", "context")),
            P(None, "tensor"),
            P(None, "tensor"),
            P(None, "tensor"),
            P(None, "tensor"),
        ),
        out_specs=(
            P(("dp", "context", "tensor"), None),
            P(("dp", "context"), "tensor"),
            P(("dp", "context"), "tensor"),
            P(("dp", "context"), "tensor"),
            P(("dp", "context"), "tensor"),
        ),
        check_vma=False,
    )
```

profile of v0, /device:TPU:0, one launch (start us, length us, event | category | flops | bytes accessed | tf_op | source)
XLA Modules:
  0.0 318.1 jit_solution(18295846007801304174)
XLA Ops:
  13.8 2.9 collective-permute-start
  18.3 10.2 %convolution_convert_fusion = bf16[512,1024]{1,0:T(8,128)(2,1)S(1)} fusion(bf16[512,5376]{1,0:T(8,128)(2,1)} %x_ref.2, bf16[5376,1024]{1,0:T(8,128)(2,1)} %param.19), kind=kOutput, calls=%fused_computation.3 | convolution fusion | flops 5637668864 | bytes 17563648 | tf_op jit(solution)/shard_map/dot_general | solution.py:653
  28.7 6.5 %pack_rows.2 = (bf16[1344,512]{1,0:T(8,128)(2,1)S(1)}, bf16[1344,256]{1,0:T(8,128)(2,1)S(1)}, bf16[1344,256]{1,0:T(8,128)(2,1)S(1)}, bf16[1344,256]{1,0:T(8,128)(2,1)S(1)}) custom-call(s32[2]{0:T(128)S(1)} %pad_add_fusion.1.at_ref.refs_0_, bf16[512,5376]{1,0:T(8,128)(2,1)} %x_ref.2), custom_call_target="tpu_custom_call" | custom-call | bytes 16515072 | tf_op jit(solution)/shard_map/pack_rows/pallas_call | solution.py:260
  35.3 5.9 %collective-permute-done.1.refs_3_ = bf16[528,512]{1,0:T(8,128)(2,1)S(1)} collective-permute-done((bf16[528,512]{1,0:T(8,128)(2,1)S(1)}, bf16[528,512]{1,0:T(8,128)(2,1)S(1)}, u32[]{:S(2)}, u32[]{:S(2)}) %collective-permute-start.1) | collective-permute-done | bytes 540704 | tf_op jit(solution)/shard_map/ppermute | solution.py:586
  45.7 3.7 %multiply_sine_fusion = (f32[2048,64]{1,0:T(8,128)S(1)}, f32[2048,64]{1,0:T(8,128)S(1)}, f32[2048,64]{1,0:T(8,128)S(1)}) fusion(f32[64]{0:T(128)S(1)} %multiply_power_fusion, f32[2048]{0:T(1024)S(1)} %add_convert_fusion.1), kind=kLoop, calls=%fused_computation.1 | loop fusion | flops 262144 | bytes 1581312 | tf_op jit(solution)/shard_map/sin | solution.py:595
  49.8 7.5 %pack_rows.3 = (bf16[1344,512]{1,0:T(8,128)(2,1)S(1)}, bf16[1344,256]{1,0:T(8,128)(2,1)}, bf16[1344,256]{1,0:T(8,128)(2,1)S(1)}, bf16[1344,256]{1,0:T(8,128)(2,1)S(1)}) custom-call(s32[2]{0:T(128)S(1)} %pad_add_fusion.1.at_ref.refs_0_, bf16[512,5376]{1,0:T(8,128)(2,1)} %x_ref.3), custom_call_target="tpu_custom_call" | custom-call | bytes 16515072 | tf_op jit(solution)/shard_map/pack_rows/pallas_call | solution.py:260
  61.2 20.4 %attention_backward.1 = (bf16[2048,384]{1,0:T(8,128)(2,1)}, bf16[2048,384]{1,0:T(8,128)(2,1)}) custom-call(s32[2]{0:T(128)S(1)} %pad_add_fusion.1.at_ref.refs_0_, bf16[528,512]{1,0:T(8,128)(2,1)S(1)} %copy-done.13, bf16[528,512]{1,0:T(8,128)(2,1)S(1)} %collective-permute-done.refs_2_, bf16[528,512]{1,0:T(8,128)(2,1)S(1)} %collective-permute-done.1.refs_3_, ...), custom_call_target="tpu_custom_call" | custom-call | flops 6710886400 | bytes 6291456 | tf_op jit(solution)/shard_map/attention_backward/pallas_call | solution.py:375
  81.6 7.5 %collective-permute-done.7.refs_3_ = bf16[1344,256]{1,0:T(8,128)(2,1)S(1)} collective-permute-done((bf16[1344,256]{1,0:T(8,128)(2,1)S(1)}, bf16[1344,256]{1,0:T(8,128)(2,1)S(1)}, u32[]{:S(2)}, u32[]{:S(2)}) %collective-permute-start.7) | collective-permute-done | bytes 688160 | tf_op jit(solution)/shard_map/ppermute | solution.py:586
  91.4 1.9 collective-permute-start.14
  94.3 6.7 %weight_terms.5 = bf16[1344,256]{1,0:T(8,128)(2,1)} custom-call(s32[2]{0:T(128)} %copy-done.8, bf16[1344,512]{1,0:T(8,128)(2,1)} %copy-done.10, bf16[1344,256]{1,0:T(8,128)(2,1)} %copy-done.19, bf16[1344,256]{1,0:T(8,128)(2,1)} %copy-done.22, bf16[1344,256]{1,0:T(8,128)(2,1)} %copy-done.20, bf16[1344,256]{1,0:T(8,128)(2,1)} %copy-done.23, ...), custom_call_target="tpu_custom_call" | custom-call | flops 8455716864 | bytes 7241728 | tf_op jit(solution)/shard_map/weight_terms/pallas_call | solution.py:437
  101.1 7.2 %collective-permute-done.12.refs_1_.refs_8_ = bf16[1344,256]{1,0:T(8,128)(2,1)} collective-permute-done((bf16[1344,256]{1,0:T(8,128)(2,1)}, bf16[1344,256]{1,0:T(8,128)(2,1)}, u32[]{:S(2)}, u32[]{:S(2)}) %collective-permute-start.12) | collective-permute-done | bytes 688160 | tf_op jit(solution)/shard_map/ppermute | solution.py:586
  108.4 14.3 %collective-permute-done.14.refs_5_.refs_12_ = bf16[1344,256]{1,0:T(8,128)(2,1)} collective-permute-done((bf16[1344,256]{1,0:T(8,128)(2,1)S(1)}, bf16[1344,256]{1,0:T(8,128)(2,1)}, u32[]{:S(2)}, u32[]{:S(2)}) %collective-permute-start.14) | collective-permute-done | bytes 688160 | tf_op jit(solution)/shard_map/ppermute | solution.py:586
  127.1 9.5 %weight_terms.6 = bf16[1344,512]{1,0:T(8,128)(2,1)} custom-call(s32[2]{0:T(128)} %copy-done.8, bf16[1344,512]{1,0:T(8,128)(2,1)} %copy-done.11, bf16[1344,256]{1,0:T(8,128)(2,1)} %collective-permute-done.12.refs_1_.refs_8_, bf16[1344,256]{1,0:T(8,128)(2,1)} %collective-permute-done.15.refs_2_.refs_9_, ...), custom_call_target="tpu_custom_call" | custom-call | flops 16911433728 | bytes 8978432 | tf_op jit(solution)/shard_map/weight_terms/pallas_call | solution.py:437
  136.7 23.5 %collective-permute-done.18.refs_14_.refs_1_ = bf16[2048,384]{1,0:T(8,128)(2,1)S(1)} collective-permute-done((bf16[2048,384]{1,0:T(8,128)(2,1)}, bf16[2048,384]{1,0:T(8,128)(2,1)S(1)}, u32[]{:S(2)}, u32[]{:S(2)}) %collective-permute-start.18) | collective-permute-done | bytes 1572896 | tf_op jit(solution)/shard_map/ppermute | solution.py:586
  163.4 11.2 %weight_terms.7 = bf16[1344,768]{1,0:T(8,128)(2,1)} custom-call(s32[2]{0:T(128)} %copy-done.8, bf16[1344,512]{1,0:T(8,128)(2,1)} %copy-done.10, bf16[1344,256]{1,0:T(8,128)(2,1)} %copy-done.19, bf16[1344,256]{1,0:T(8,128)(2,1)} %copy-done.22, bf16[1344,256]{1,0:T(8,128)(2,1)} %copy-done.20, bf16[1344,256]{1,0:T(8,128)(2,1)} %copy-done.23, ...), custom_call_target="tpu_custom_call" | custom-call | flops 84557168640 | bytes 16220160 | tf_op jit(solution)/shard_map/weight_terms/pallas_call | solution.py:437
  174.6 22.9 %collective-permute-done.20.refs_14_.refs_2_ = bf16[2048,384]{1,0:T(8,128)(2,1)} collective-permute-done((bf16[2048,384]{1,0:T(8,128)(2,1)}, bf16[2048,384]{1,0:T(8,128)(2,1)}, u32[]{:S(2)}, u32[]{:S(2)}) %collective-permute-start.20) | collective-permute-done | bytes 1572896 | tf_op jit(solution)/shard_map/ppermute | solution.py:586
  199.9 11.2 %weight_terms.8 = bf16[1344,768]{1,0:T(8,128)(2,1)} custom-call(s32[2]{0:T(128)} %copy-done.8, bf16[1344,512]{1,0:T(8,128)(2,1)} %copy-done.10, bf16[1344,256]{1,0:T(8,128)(2,1)} %copy-done.19, bf16[1344,256]{1,0:T(8,128)(2,1)} %copy-done.22, bf16[1344,256]{1,0:T(8,128)(2,1)} %copy-done.20, bf16[1344,256]{1,0:T(8,128)(2,1)} %copy-done.23, ...), custom_call_target="tpu_custom_call" | custom-call | flops 84557168640 | bytes 16220160 | tf_op jit(solution)/shard_map/weight_terms/pallas_call | solution.py:437
  211.2 19.9 %input_first.1.part_ref = f32[512,5376]{1,0:T(8,128)} custom-call(s32[2]{0:T(128)} %copy-done.8, bf16[2048,384]{1,0:T(8,128)(2,1)} %get-tuple-element.175.refs_7_.refs_0_, bf16[2048,384]{1,0:T(8,128)(2,1)} %copy-done.14, bf16[2048,384]{1,0:T(8,128)(2,1)} %collective-permute-done.20.refs_14_.refs_2_, bf16[2048,384]{1,0:T(8,128)(2,1)} %get-tuple-element.176.refs_8_.refs_3_, ...), custom_call_target="tpu_custom_call" | custom-call | flops 5637144576 | tf_op jit(solution)/shard_map/input_first/pallas_call | solution.py:525
  235.0 14.9 %input_last.1 = (f32[256,5376]{1,0:T(8,128)}, bf16[256,5376]{1,0:T(8,128)(2,1)}) custom-call(s32[2]{0:T(128)} %copy-done.8, bf16[2048,384]{1,0:T(8,128)(2,1)} %copy-done.17, bf16[2048,384]{1,0:T(8,128)(2,1)} %copy-done.18, bf16[5376,1024]{1,0:T(8,128)(2,1)} %wq_ref.1, bf16[5376,512]{1,0:T(8,128)(2,1)} %wk_ref.1, bf16[5376,512]{1,0:T(8,128)(2,1)} %wv_ref.1, ...), custom_call_target="tpu_custom_call" | custom-call | flops 112742891520 | tf_op jit(solution)/shard_map/input_last/pallas_call | solution.py:562
  249.9 11.2 %weight_terms.9 = bf16[1344,768]{1,0:T(8,128)(2,1)} custom-call(s32[2]{0:T(128)} %copy-done.8, bf16[1344,512]{1,0:T(8,128)(2,1)} %copy-done.10, bf16[1344,256]{1,0:T(8,128)(2,1)} %copy-done.19, bf16[1344,256]{1,0:T(8,128)(2,1)} %copy-done.22, bf16[1344,256]{1,0:T(8,128)(2,1)} %copy-done.20, bf16[1344,256]{1,0:T(8,128)(2,1)} %copy-done.23, ...), custom_call_target="tpu_custom_call" | custom-call | flops 84557168640 | bytes 16220160 | tf_op jit(solution)/shard_map/weight_terms/pallas_call | solution.py:437
  261.2 1.8 reduce-scatter.12.cloned.1.call-done.refs_3_
  263.0 5.5 %add_convert_fusion = bf16[256,5376]{1,0:T(8,128)(2,1)} fusion(f32[256,5376]{1,0:T(8,128)} %get-tuple-element.188, bf16[256,5376]{1,0:T(8,128)(2,1)} %collective-permute-done.24), kind=kLoop, calls=%fused_computation | loop fusion | flops 4128768 | bytes 11010048 | tf_op jit(solution)/shard_map/convert_element_type | solution.py:741
  268.4 39.2 %reduce-scatter.14.cloned.1.call-done.refs_4_ = bf16[336,768]{1,0:T(8,128)(2,1)} async-done(((bf16[1344,768]{1,0:T(8,128)(2,1)}), bf16[336,768]{1,0:T(8,128)(2,1)}) %reduce-scatter.14.cloned.1.call-update) | async-done | bytes 516112 | tf_op jit(solution)/shard_map/reduce_scatter | solution.py:692
  308.7 2.8 assemble.1
  (123 shorter events, 35.7 us)
Async XLA Ops:
  7.2 119.9 %reduce-scatter.6.cloned.1.call-start = ((), (), s32[]{:S(2)}) async-start(), calls=%async_computation.5 | async-start | bytes 860160 | tf_op jit(solution)/shard_map/reduce_scatter | solution.py:692
  13.8 21.4 %collective-permute-start = (bf16[528,512]{1,0:T(8,128)(2,1)}, bf16[528,512]{1,0:T(8,128)(2,1)S(1)}, u32[]{:S(2)}, u32[]{:S(2)}) collective-permute-start(bf16[528,512]{1,0:T(8,128)(2,1)} %get-tuple-element.114), channel_id=1, source_target_pairs={{0,2},{2,0},{4,6},{6,4},{1,3},{3,1},{5,7},{7,5},{8,10},{10,8},{12,... | collective-permute-start | bytes 1622024 | tf_op jit(solution)/shard_map/ppermute | solution.py:586
  16.8 24.4 %collective-permute-start.1 = (bf16[528,512]{1,0:T(8,128)(2,1)S(1)}, bf16[528,512]{1,0:T(8,128)(2,1)S(1)}, u32[]{:S(2)}, u32[]{:S(2)}) collective-permute-start(bf16[528,512]{1,0:T(8,128)(2,1)S(1)} %get-tuple-element.115), channel_id=1, source_target_pairs={{0,4},{2,6},{4,0},{6,2},{1,5},{3,7},{5,1},{7,3},{8,12},{10,14},{12... | collective-permute-start | bytes 1622024 | tf_op jit(solution)/shard_map/ppermute | solution.py:586
  18.3 23.8 %collective-permute-start.2 = (bf16[528,512]{1,0:T(8,128)(2,1)S(1)}, bf16[528,512]{1,0:T(8,128)(2,1)S(1)}, u32[]{:S(2)}, u32[]{:S(2)}) collective-permute-start(bf16[528,512]{1,0:T(8,128)(2,1)S(1)} %get-tuple-element.116), channel_id=1, source_target_pairs={{0,6},{2,4},{4,2},{6,0},{1,7},{3,5},{5,3},{7,1},{8,14},{10,12},{12... | collective-permute-start | bytes 1622024 | tf_op jit(solution)/shard_map/ppermute | solution.py:586
  42.1 15.5 %collective-permute-start.3 = (bf16[512,256]{1,0:T(8,128)(2,1)S(1)}, bf16[512,256]{1,0:T(8,128)(2,1)S(1)}, u32[]{:S(2)}, u32[]{:S(2)}) collective-permute-start(bf16[512,256]{1,0:T(8,128)(2,1)S(1)} %get-tuple-element.130), channel_id=1, source_target_pairs={{0,2},{2,0},{4,6},{6,4},{1,3},{3,1},{5,7},{7,5},{8,10},{10,8},{12,... | collective-permute-start | bytes 786440 | tf_op jit(solution)/shard_map/ppermute | solution.py:586
  43.6 14.0 %collective-permute-start.4 = (bf16[512,256]{1,0:T(8,128)(2,1)S(1)}, bf16[512,256]{1,0:T(8,128)(2,1)S(1)}, u32[]{:S(2)}, u32[]{:S(2)}) collective-permute-start(bf16[512,256]{1,0:T(8,128)(2,1)S(1)} %get-tuple-element.131), channel_id=1, source_target_pairs={{0,4},{2,6},{4,0},{6,2},{1,5},{3,7},{5,1},{7,3},{8,12},{10,14},{12... | collective-permute-start | bytes 786440 | tf_op jit(solution)/shard_map/ppermute | solution.py:586
  44.2 13.4 %collective-permute-start.5 = (bf16[512,256]{1,0:T(8,128)(2,1)S(1)}, bf16[512,256]{1,0:T(8,128)(2,1)S(1)}, u32[]{:S(2)}, u32[]{:S(2)}) collective-permute-start(bf16[512,256]{1,0:T(8,128)(2,1)S(1)} %get-tuple-element.132), channel_id=1, source_target_pairs={{0,6},{2,4},{4,2},{6,0},{1,7},{3,5},{5,3},{7,1},{8,14},{10,12},{12... | collective-permute-start | bytes 786440 | tf_op jit(solution)/shard_map/ppermute | solution.py:586
  57.7 24.0 %collective-permute-start.6 = (bf16[1344,256]{1,0:T(8,128)(2,1)S(1)}, bf16[1344,256]{1,0:T(8,128)(2,1)S(1)}, u32[]{:S(2)}, u32[]{:S(2)}) collective-permute-start(bf16[1344,256]{1,0:T(8,128)(2,1)S(1)} %get-tuple-element.146), channel_id=1, source_target_pairs={{0,2},{2,0},{4,6},{6,4},{1,3},{3,1},{5,7},{7,5},{8,10},{10,8},{12,... | collective-permute-start | bytes 2064392 | tf_op jit(solution)/shard_map/ppermute | solution.py:586
  59.2 29.9 %collective-permute-start.7 = (bf16[1344,256]{1,0:T(8,128)(2,1)S(1)}, bf16[1344,256]{1,0:T(8,128)(2,1)S(1)}, u32[]{:S(2)}, u32[]{:S(2)}) collective-permute-start(bf16[1344,256]{1,0:T(8,128)(2,1)S(1)} %get-tuple-element.147), channel_id=1, source_target_pairs={{0,4},{2,6},{4,0},{6,2},{1,5},{3,7},{5,1},{7,3},{8,12},{10,14},{12... | collective-permute-start | bytes 2064392 | tf_op jit(solution)/shard_map/ppermute | solution.py:586
  59.8 29.3 %collective-permute-start.8 = (bf16[1344,256]{1,0:T(8,128)(2,1)S(1)}, bf16[1344,256]{1,0:T(8,128)(2,1)S(1)}, u32[]{:S(2)}, u32[]{:S(2)}) collective-permute-start(bf16[1344,256]{1,0:T(8,128)(2,1)S(1)} %get-tuple-element.148), channel_id=1, source_target_pairs={{0,6},{2,4},{4,2},{6,0},{1,7},{3,5},{5,3},{7,1},{8,14},{10,12},{12... | collective-permute-start | bytes 2064392 | tf_op jit(solution)/shard_map/ppermute | solution.py:586
  89.8 18.6 %collective-permute-start.12 = (bf16[1344,256]{1,0:T(8,128)(2,1)}, bf16[1344,256]{1,0:T(8,128)(2,1)}, u32[]{:S(2)}, u32[]{:S(2)}) collective-permute-start(bf16[1344,256]{1,0:T(8,128)(2,1)} %get-tuple-element.157), channel_id=1, source_target_pairs={{0,2},{2,0},{4,6},{6,4},{1,3},{3,1},{5,7},{7,5},{8,10},{10,8},{12,... | collective-permute-start | bytes 2064392 | tf_op jit(solution)/shard_map/ppermute | solution.py:586
  90.3 18.1 %collective-permute-start.13 = (bf16[1344,256]{1,0:T(8,128)(2,1)S(1)}, bf16[1344,256]{1,0:T(8,128)(2,1)}, u32[]{:S(2)}, u32[]{:S(2)}) collective-permute-start(bf16[1344,256]{1,0:T(8,128)(2,1)S(1)} %get-tuple-element.158), channel_id=1, source_target_pairs={{0,4},{2,6},{4,0},{6,2},{1,5},{3,7},{5,1},{7,3},{8,12},{10,14},{12... | collective-permute-start | bytes 2064392 | tf_op jit(solution)/shard_map/ppermute | solution.py:586
  91.4 31.3 %collective-permute-start.14 = (bf16[1344,256]{1,0:T(8,128)(2,1)S(1)}, bf16[1344,256]{1,0:T(8,128)(2,1)}, u32[]{:S(2)}, u32[]{:S(2)}) collective-permute-start(bf16[1344,256]{1,0:T(8,128)(2,1)S(1)} %get-tuple-element.159), channel_id=1, source_target_pairs={{0,6},{2,4},{4,2},{6,0},{1,7},{3,5},{5,3},{7,1},{8,14},{10,12},{12... | collective-permute-start | bytes 2064392 | tf_op jit(solution)/shard_map/ppermute | solution.py:586
  101.1 130.0 %reduce-scatter.8.cloned.1.call-start = ((), (), s32[]{:S(2)}) async-start(), calls=%async_computation.6 | async-start | bytes 1720320 | tf_op jit(solution)/shard_map/reduce_scatter | solution.py:692
  123.2 37.0 %collective-permute-start.18 = (bf16[2048,384]{1,0:T(8,128)(2,1)}, bf16[2048,384]{1,0:T(8,128)(2,1)S(1)}, u32[]{:S(2)}, u32[]{:S(2)}) collective-permute-start(bf16[2048,384]{1,0:T(8,128)(2,1)} %get-tuple-element.175.refs_7_.refs_0_), channel_id=1, source_target_pairs={{0,2},{2,0},{4,6},{6,4},{1,3},{3,1},{5,7},{7,5},{8,10},{10,8},{12,... | collective-permute-start | bytes 4718600 | tf_op jit(solution)/shard_map/ppermute | solution.py:586
  124.7 36.7 %collective-permute-start.19 = (bf16[2048,384]{1,0:T(8,128)(2,1)}, bf16[2048,384]{1,0:T(8,128)(2,1)S(1)}, u32[]{:S(2)}, u32[]{:S(2)}) collective-permute-start(bf16[2048,384]{1,0:T(8,128)(2,1)} %get-tuple-element.176.refs_8_.refs_3_), channel_id=1, source_target_pairs={{0,4},{2,6},{4,0},{6,2},{1,5},{3,7},{5,1},{7,3},{8,12},{10,14},{12... | collective-permute-start | bytes 4718600 | tf_op jit(solution)/shard_map/ppermute | solution.py:586
  136.7 124.5 %reduce-scatter.10.cloned.1.call-start = ((), (), s32[]{:S(2)}) async-start(), calls=%async_computation.7 | async-start | bytes 2580480 | tf_op jit(solution)/shard_map/reduce_scatter | solution.py:692
  161.4 36.1 %collective-permute-start.20 = (bf16[2048,384]{1,0:T(8,128)(2,1)}, bf16[2048,384]{1,0:T(8,128)(2,1)}, u32[]{:S(2)}, u32[]{:S(2)}) collective-permute-start(bf16[2048,384]{1,0:T(8,128)(2,1)} %get-tuple-element.175.refs_7_.refs_0_), channel_id=1, source_target_pairs={{0,4},{2,6},{4,0},{6,2},{1,5},{3,7},{5,1},{7,3},{8,12},{10,14},{12... | collective-permute-start | bytes 4718600 | tf_op jit(solution)/shard_map/ppermute | solution.py:586
  161.9 35.9 %collective-permute-start.21 = (bf16[2048,384]{1,0:T(8,128)(2,1)}, bf16[2048,384]{1,0:T(8,128)(2,1)}, u32[]{:S(2)}, u32[]{:S(2)}) collective-permute-start(bf16[2048,384]{1,0:T(8,128)(2,1)} %get-tuple-element.176.refs_8_.refs_3_), channel_id=1, source_target_pairs={{0,2},{2,0},{4,6},{6,4},{1,3},{3,1},{5,7},{7,5},{8,10},{10,8},{12,... | collective-permute-start | bytes 4718600 | tf_op jit(solution)/shard_map/ppermute | solution.py:586
  174.6 88.4 %reduce-scatter.12.cloned.1.call-start = ((), (), s32[]{:S(2)}) async-start(), calls=%async_computation.8 | async-start | bytes 2580480 | tf_op jit(solution)/shard_map/reduce_scatter | solution.py:692
  197.8 34.9 %collective-permute-start.22 = (bf16[2048,384]{1,0:T(8,128)(2,1)}, bf16[2048,384]{1,0:T(8,128)(2,1)S(1)}, u32[]{:S(2)}, u32[]{:S(2)}) collective-permute-start(bf16[2048,384]{1,0:T(8,128)(2,1)} %copy-done.14), channel_id=1, source_target_pairs={{0,4},{2,6},{4,0},{6,2},{1,5},{3,7},{5,1},{7,3},{8,12},{10,14},{12... | collective-permute-start | bytes 4718600 | tf_op jit(solution)/shard_map/ppermute | solution.py:586
  199.3 34.5 %collective-permute-start.23 = (bf16[2048,384]{1,0:T(8,128)(2,1)}, bf16[2048,384]{1,0:T(8,128)(2,1)S(1)}, u32[]{:S(2)}, u32[]{:S(2)}) collective-permute-start(bf16[2048,384]{1,0:T(8,128)(2,1)} %copy-done.15), channel_id=1, source_target_pairs={{0,2},{2,0},{4,6},{6,4},{1,3},{3,1},{5,7},{7,5},{8,10},{10,8},{12,... | collective-permute-start | bytes 4718600 | tf_op jit(solution)/shard_map/ppermute | solution.py:586
  211.2 96.5 %reduce-scatter.14.cloned.1.call-start = ((), (), s32[]{:S(2)}) async-start(), calls=%async_computation.9 | async-start | bytes 2580480 | tf_op jit(solution)/shard_map/reduce_scatter | solution.py:692
  249.8 13.1 %collective-permute-start.24 = (bf16[256,5376]{1,0:T(8,128)(2,1)}, bf16[256,5376]{1,0:T(8,128)(2,1)}, u32[]{:S(2)}, u32[]{:S(2)}) collective-permute-start(bf16[256,5376]{1,0:T(8,128)(2,1)} %get-tuple-element.187), channel_id=1, source_target_pairs={{0,1},{1,0},{2,3},{3,2},{4,5},{5,4},{6,7},{7,6},{8,9},{9,8},{10,11... | collective-permute-start | bytes 8257544 | tf_op jit(solution)/shard_map/ppermute | solution.py:586
  (31 other events, 379.6 us)
Sparse Core Ops, SparseCore 0:
  101.2 22.3 reduce-scatter.5
  136.8 32.5 reduce-scatter.7
  174.7 43.4 reduce-scatter.9
  220.5 42.4 reduce-scatter.11
  265.2 42.4 reduce-scatter.13
where the time goes:
time: 319 us; the launch traced here: 318 us
  waiting for transfers between devices  129 us (40%)
  Pallas kernels  123 us (39%)
  starting transfers between devices  22.5 us (7%)
  between operations  14.1 us (4%)
  other arithmetic  10.7 us (3%)
  matrix products  10.2 us (3%)
  local copies, waits for them, and re-layouts  7.57 us (2%)
    ppermute x25, waiting for transfers between devices, swap(): return lax.ppermute(x, axis, [(i, i ^ by) for i in range(count)])  88.3 us
    pallas_call x5, Pallas kernels, weight_terms(): pl.pallas_call(functools.partial(weight_terms_kernel, blocks, jobs), out_...  49.8 us
    reduce_scatter x5, waiting for transfers between devices, summed(): return lax.psum_scatter(term, 'dp', scatter_dimension=0, tiled=True)  41.1 us
    ppermute x25, starting transfers between devices, swap(): return lax.ppermute(x, axis, [(i, i ^ by) for i in range(count)])  22.3 us
    pallas_call x1, Pallas kernels, attention(): pl.pallas_call(functools.partial(attention_kernel, blocks, count, heads,...  20.4 us
    pallas_call x1, Pallas kernels, input_first(): pl.pallas_call(functools.partial(input_first_kernel, blocks, wide, narrow...  19.9 us
    pallas_call x1, Pallas kernels, input_last(): pl.pallas_call(functools.partial(input_last_kernel, wide), out_shape=(jax...  14.9 us
    pallas_call x2, Pallas kernels, pack_rows(): pl.pallas_call(functools.partial(pack_rows_kernel, blocks, replicas, rows...  14 us
  transfers between devices with their start and end apart: 30, of which 16 were waited for; matrix products, arithmetic and copies ran while one was open for 6% of the time, Pallas kernels for 37%

commit v1 on v0

--- a/solution.py
+++ b/solution.py
@@ -221,9 +221,9 @@
     return pl.pallas_call(
         functools.partial(pack_heads_kernel, blocks, wide, narrow),
         out_shape=(shape,) * blocks,
-        in_specs=[scalars()] + [whole()] * 4,
+        in_specs=[scalars()] + [pl.BlockSpec(x.shape, lambda: (0, 0)) for x in (queries, key_states, value_states, extra)],
         out_specs=(whole(),) * blocks,
-        compiler_params=params(),
+        compiler_params=params(VMEM_MOST),
         cost_estimate=pl.CostEstimate(
             flops=0, bytes_accessed=4 * blocks * count * (wide + 2 * narrow), transcendentals=0
         ),
@@ -237,12 +237,14 @@
     count, width = x_ref.shape
     half = count // 2
 
+    step = next(n for n in (6, 3, 2, 1) if width % (n * HD) == 0) * HD
+
     def turn(index, carry):
-        cols = aligned(index, HD)
+        cols = aligned(index, step)
         turned[cols, :] = x_ref[:, cols].T
         return carry
 
-    lax.fori_loop(0, width // HD, turn, 0)
+    lax.fori_loop(0, width // step, turn, 0)
     for replica in range(replicas):
         into = pl.ds(replica * rows, rows)
         own_ref[into, :] = turned[aligned(replica * blocks + me, rows), :]
@@ -481,6 +483,43 @@
     )(at, *parts)
 
 
+def assemble_last_kernel(places, at_ref, part_ref, *refs):
+    outs, wide_s, sems = refs[4:8], refs[8], refs[9]
+    me = at_ref[0]
+    wide_s[...] = part_ref[...].astype(jnp.float32)
+    copies = []
+    first = 0
+    for index, (out, source, cols) in enumerate(places):
+        copies.append(
+            pltpu.make_async_copy(
+                wide_s.at[:, first : first + cols],
+                outs[out].at[:, aligned(me ^ source, cols)],
+                sems.at[index],
+            )
+        )
+        copies[-1].start()
+        first += cols
+    for copy in copies:
+        copy.wait()
+
+
+def assemble_last(at, places, part, grads):
+    anywhere = pl.BlockSpec(memory_space=pl.ANY)
+    return pl.pallas_call(
+        functools.partial(assemble_last_kernel, places),
+        out_shape=tuple(jax.ShapeDtypeStruct(x.shape, x.dtype) for x in grads),
+        in_specs=[scalars(), whole()] + [anywhere] * 4,
+        out_specs=(anywhere,) * 4,
+        scratch_shapes=[
+            pltpu.VMEM(part.shape, jnp.float32),
+            pltpu.SemaphoreType.DMA((len(places),)),
+        ],
+        input_output_aliases={2: 0, 3: 1, 4: 2, 5: 3},
+        compiler_params=params(),
+        name="assemble_last",
+    )(at, part, *grads)
+
+
 def input_first_kernel(blocks, wide, narrow, at_ref, *refs):
     firsts, seconds = refs[: blocks - 1], refs[blocks - 1 : 2 * (blocks - 1)]
     wq_ref, wk_ref, wv_ref, out_ref, q_s, k_s, v_s = refs[2 * (blocks - 1) :]
@@ -664,8 +703,10 @@
         return pieces
 
     soon, dpacks = barrier((at, dpacks))
-    packs, dpacks = barrier((packs, dpacks))
     grad_own, *grad_packed = pack_rows(soon, out_grad, blocks, replicas)
+    soon, grad_packed = barrier((soon, grad_packed))
+    input_own, *input_packed = pack_rows(soon, inputs, blocks, replicas)
+    packs, dpacks, grad_packed, input_packed = barrier((packs, dpacks, grad_packed, input_packed))
     dpacks = [dpacks[0]] + spread(dpacks[1:])
     places = [
         (pack[count, :count].astype(jnp.float32) * RADIX + pack[count + 1, :count].astype(jnp.float32)).astype(jnp.int32)
@@ -677,10 +718,6 @@
     )
     low = jnp.maximum(index - places, index - (W - 1))[None, :]
     cosine, sine = rotation_tables(places)
-    soon, grad_packed, packs = barrier((soon, grad_packed, packs))
-    input_own, *input_packed = pack_rows(soon, inputs, blocks, replicas)
-    dpacks, grad_packed, input_packed = barrier((dpacks, grad_packed, input_packed))
-
     grad_came = spread(grad_packed)
     first, second = attention(at, packs, dpacks, low, cosine, sine, heads, group)
     first, second, grad_came, input_packed = barrier((first, second, grad_came, input_packed))
@@ -747,9 +784,8 @@
     layout = [[(0, 0, wide)], rest(0, 0)]
     for source_first, source_second in ((1, 2), (2, 1), (3, 3)):
         layout.append([(0, source_first, wide)] + rest(source_first, source_second))
-    grad_output, grad_value, grad_query, grad_key = assemble(
-        last, layout, parts, blocks, wide, narrow
-    )
+    near = assemble(last, layout[:-1], parts[:-1], blocks, wide, narrow)
+    grad_output, grad_value, grad_query, grad_key = assemble_last(at, layout[-1], parts[-1], near)
     return (input_grad, grad_query, grad_key, grad_value, grad_output)
 
 

time: 319 us -> 313 us (0.981)
    pallas_call x2, Pallas kernels: 14 us -> 10.2 us  [pack_rows(): pl.pallas_call(functools.partial(pack_rows_kernel, blocks, replicas, rows...]
    unnamed x50 -> x42, local copies, waits for them, and re-layouts: 7.41 us -> 4.39 us
  transfers between devices with their start and end apart: 30 -> 30, of which waited for: 16 -> 17; matrix products, arithmetic and copies ran while one was open for 6% -> 7% of each run, Pallas kernels for 37% -> 38%
where the time goes in v1:
time: 313 us; the launch traced here: 312 us
  waiting for transfers between devices  126 us (40%)
  Pallas kernels  123 us (39%)
  starting transfers between devices  22.5 us (7%)
  between operations  14.1 us (5%)
  other arithmetic  11.8 us (4%)
  matrix products  10.2 us (3%)
  local copies, waits for them, and re-layouts  4.55 us (1%)
    ppermute x25, waiting for transfers between devices, swap(): return lax.ppermute(x, axis, [(i, i ^ by) for i in range(count)])  87.3 us
    pallas_call x5, Pallas kernels, weight_terms(): pl.pallas_call(functools.partial(weight_terms_kernel, blocks, jobs), out_...  49.6 us
    reduce_scatter x5, waiting for transfers between devices, summed(): return lax.psum_scatter(term, 'dp', scatter_dimension=0, tiled=True)  38.3 us
    ppermute x25, starting transfers between devices, swap(): return lax.ppermute(x, axis, [(i, i ^ by) for i in range(count)])  22.3 us
    pallas_call x1, Pallas kernels, attention(): pl.pallas_call(functools.partial(attention_kernel, blocks, count, heads,...  20.7 us
    pallas_call x1, Pallas kernels, input_first(): pl.pallas_call(functools.partial(input_first_kernel, blocks, wide, narrow...  20.1 us
    pallas_call x1, Pallas kernels, input_last(): pl.pallas_call(functools.partial(input_last_kernel, wide), out_shape=(jax...  14.9 us
    dot_general x1, matrix products, on_device(): jnp.dot(after, w_output, preferred_element_type=jnp.float32)  10.2 us
  transfers between devices with their start and end apart: 30, of which 17 were waited for; matrix products, arithmetic and copies ran while one was open for 7% of the time, Pallas kernels for 38%

profile of v1, /device:TPU:0, one launch (start us, length us, event | category | flops | bytes accessed | tf_op | source)
XLA Modules:
  0.0 311.7 jit_solution(6773517181688000507)
XLA Ops:
  9.1 3.1 pack_heads.1
  12.2 3.0 collective-permute-start
  16.7 10.2 %convolution_convert_fusion = bf16[512,1024]{1,0:T(8,128)(2,1)S(1)} fusion(bf16[512,5376]{1,0:T(8,128)(2,1)} %x_ref.2, bf16[5376,1024]{1,0:T(8,128)(2,1)} %param.19), kind=kOutput, calls=%fused_computation.3 | convolution fusion | flops 5637668864 | bytes 17563648 | tf_op jit(solution)/shard_map/dot_general | solution.py:692
  27.1 4.6 %pack_rows.2 = (bf16[1344,512]{1,0:T(8,128)(2,1)S(1)}, bf16[1344,256]{1,0:T(8,128)(2,1)S(1)}, bf16[1344,256]{1,0:T(8,128)(2,1)S(1)}, bf16[1344,256]{1,0:T(8,128)(2,1)S(1)}) custom-call(s32[2]{0:T(128)S(1)} %copy-done.5, bf16[512,5376]{1,0:T(8,128)(2,1)} %x_ref.2), custom_call_target="tpu_custom_call" | custom-call | bytes 16515072 | tf_op jit(solution)/shard_map/pack_rows/pallas_call | solution.py:262
  32.7 5.6 %pack_rows.3 = (bf16[1344,512]{1,0:T(8,128)(2,1)S(1)}, bf16[1344,256]{1,0:T(8,128)(2,1)}, bf16[1344,256]{1,0:T(8,128)(2,1)S(1)}, bf16[1344,256]{1,0:T(8,128)(2,1)S(1)}) custom-call(s32[2]{0:T(128)S(1)} %copy-done.5, bf16[512,5376]{1,0:T(8,128)(2,1)} %x_ref.3), custom_call_target="tpu_custom_call" | custom-call | bytes 16515072 | tf_op jit(solution)/shard_map/pack_rows/pallas_call | solution.py:262
  38.4 2.2 collective-permute-done.1.refs_3_
  46.3 3.7 %multiply_sine_fusion = (f32[2048,64]{1,0:T(8,128)S(1)}, f32[2048,64]{1,0:T(8,128)S(1)}, f32[2048,64]{1,0:T(8,128)S(1)}) fusion(f32[64]{0:T(128)S(1)} %multiply_power_fusion, f32[2048]{0:T(1024)S(1)} %add_convert_fusion.1), kind=kLoop, calls=%fused_computation.1 | loop fusion | flops 262144 | bytes 1581312 | tf_op jit(solution)/shard_map/sin | solution.py:634
  52.3 3.8 %collective-permute-done.4.refs_7_ = bf16[512,256]{1,0:T(8,128)(2,1)S(1)} collective-permute-done((bf16[512,256]{1,0:T(8,128)(2,1)S(1)}, bf16[512,256]{1,0:T(8,128)(2,1)S(1)}, u32[]{:S(2)}, u32[]{:S(2)}) %collective-permute-start.4) | collective-permute-done | bytes 262176 | tf_op jit(solution)/shard_map/ppermute | solution.py:625
  56.6 20.7 %attention_backward.1 = (bf16[2048,384]{1,0:T(8,128)(2,1)}, bf16[2048,384]{1,0:T(8,128)(2,1)}) custom-call(s32[2]{0:T(128)S(1)} %copy-done.5, bf16[528,512]{1,0:T(8,128)(2,1)S(1)} %copy-done.9, bf16[528,512]{1,0:T(8,128)(2,1)S(1)} %collective-permute-done.refs_2_, bf16[528,512]{1,0:T(8,128)(2,1)S(1)} %collective-permute-done.1.refs_3_, ...), custom_call_target="tpu_custom_call" | custom-call | flops 6710886400 | bytes 6291456 | tf_op jit(solution)/shard_map/attention_backward/pallas_call | solution.py:377
  77.3 6.7 %collective-permute-done.7.refs_3_ = bf16[1344,256]{1,0:T(8,128)(2,1)S(1)} collective-permute-done((bf16[1344,256]{1,0:T(8,128)(2,1)S(1)}, bf16[1344,256]{1,0:T(8,128)(2,1)S(1)}, u32[]{:S(2)}, u32[]{:S(2)}) %collective-permute-start.7) | collective-permute-done | bytes 688160 | tf_op jit(solution)/shard_map/ppermute | solution.py:625
  89.2 6.7 %weight_terms.5 = bf16[1344,256]{1,0:T(8,128)(2,1)} custom-call(s32[2]{0:T(128)} %pad_add_fusion.1.at_ref.refs_0_, bf16[1344,512]{1,0:T(8,128)(2,1)} %copy-done.7, bf16[1344,256]{1,0:T(8,128)(2,1)} %copy-done.15, bf16[1344,256]{1,0:T(8,128)(2,1)} %copy-done.18, bf16[1344,256]{1,0:T(8,128)(2,1)} %copy-done.16, bf16[1344,256]{1,0:T(8,128)(2,1)} %copy-done.19, ...), custom_call_target="tpu_custom_call" | custom-call | flops 8455716864 | bytes 7241728 | tf_op jit(solution)/shard_map/weight_terms/pallas_call | solution.py:439
  96.0 7.2 %collective-permute-done.12.refs_1_.refs_8_ = bf16[1344,256]{1,0:T(8,128)(2,1)} collective-permute-done((bf16[1344,256]{1,0:T(8,128)(2,1)}, bf16[1344,256]{1,0:T(8,128)(2,1)}, u32[]{:S(2)}, u32[]{:S(2)}) %collective-permute-start.12) | collective-permute-done | bytes 688160 | tf_op jit(solution)/shard_map/ppermute | solution.py:625
  103.3 14.3 %collective-permute-done.14.refs_5_.refs_12_ = bf16[1344,256]{1,0:T(8,128)(2,1)} collective-permute-done((bf16[1344,256]{1,0:T(8,128)(2,1)S(1)}, bf16[1344,256]{1,0:T(8,128)(2,1)}, u32[]{:S(2)}, u32[]{:S(2)}) %collective-permute-start.14) | collective-permute-done | bytes 688160 | tf_op jit(solution)/shard_map/ppermute | solution.py:625
  122.0 9.3 %weight_terms.6 = bf16[1344,512]{1,0:T(8,128)(2,1)} custom-call(s32[2]{0:T(128)} %pad_add_fusion.1.at_ref.refs_0_, bf16[1344,512]{1,0:T(8,128)(2,1)} %copy-done.8, bf16[1344,256]{1,0:T(8,128)(2,1)} %collective-permute-done.12.refs_1_.refs_8_, bf16[1344,256]{1,0:T(8,128)(2,1)} %collective-permute-done.15.refs_2_.refs_9_, ...), custom_call_target="tpu_custom_call" | custom-call | flops 16911433728 | bytes 8978432 | tf_op jit(solution)/shard_map/weight_terms/pallas_call | solution.py:439
  131.4 23.7 %collective-permute-done.18.refs_14_.refs_1_ = bf16[2048,384]{1,0:T(8,128)(2,1)S(1)} collective-permute-done((bf16[2048,384]{1,0:T(8,128)(2,1)}, bf16[2048,384]{1,0:T(8,128)(2,1)S(1)}, u32[]{:S(2)}, u32[]{:S(2)}) %collective-permute-start.18) | collective-permute-done | bytes 1572896 | tf_op jit(solution)/shard_map/ppermute | solution.py:625
  158.2 11.2 %weight_terms.7 = bf16[1344,768]{1,0:T(8,128)(2,1)} custom-call(s32[2]{0:T(128)} %pad_add_fusion.1.at_ref.refs_0_, bf16[1344,512]{1,0:T(8,128)(2,1)} %copy-done.7, bf16[1344,256]{1,0:T(8,128)(2,1)} %copy-done.15, bf16[1344,256]{1,0:T(8,128)(2,1)} %copy-done.18, bf16[1344,256]{1,0:T(8,128)(2,1)} %copy-done.16, bf16[1344,256]{1,0:T(8,128)(2,1)} %copy-done.19, ...), custom_call_target="tpu_custom_call" | custom-call | flops 84557168640 | bytes 16220160 | tf_op jit(solution)/shard_map/weight_terms/pallas_call | solution.py:439
  169.5 22.9 %collective-permute-done.20.refs_14_.refs_2_ = bf16[2048,384]{1,0:T(8,128)(2,1)} collective-permute-done((bf16[2048,384]{1,0:T(8,128)(2,1)}, bf16[2048,384]{1,0:T(8,128)(2,1)}, u32[]{:S(2)}, u32[]{:S(2)}) %collective-permute-start.20) | collective-permute-done | bytes 1572896 | tf_op jit(solution)/shard_map/ppermute | solution.py:625
  194.8 11.2 %weight_terms.8 = bf16[1344,768]{1,0:T(8,128)(2,1)} custom-call(s32[2]{0:T(128)} %pad_add_fusion.1.at_ref.refs_0_, bf16[1344,512]{1,0:T(8,128)(2,1)} %copy-done.7, bf16[1344,256]{1,0:T(8,128)(2,1)} %copy-done.15, bf16[1344,256]{1,0:T(8,128)(2,1)} %copy-done.18, bf16[1344,256]{1,0:T(8,128)(2,1)} %copy-done.16, bf16[1344,256]{1,0:T(8,128)(2,1)} %copy-done.19, ...), custom_call_target="tpu_custom_call" | custom-call | flops 84557168640 | bytes 16220160 | tf_op jit(solution)/shard_map/weight_terms/pallas_call | solution.py:439
  206.1 20.1 %input_first.1.part_ref = f32[512,5376]{1,0:T(8,128)} custom-call(s32[2]{0:T(128)} %pad_add_fusion.1.at_ref.refs_0_, bf16[2048,384]{1,0:T(8,128)(2,1)} %get-tuple-element.163.refs_7_.refs_0_, bf16[2048,384]{1,0:T(8,128)(2,1)} %copy-done.10, bf16[2048,384]{1,0:T(8,128)(2,1)} %collective-permute-done.20.refs_14_.refs_2_, ...), custom_call_target="tpu_custom_call" | custom-call | flops 5637144576 | tf_op jit(solution)/shard_map/input_first/pallas_call | solution.py:564
  229.9 14.9 %input_last.1 = (f32[256,5376]{1,0:T(8,128)}, bf16[256,5376]{1,0:T(8,128)(2,1)}) custom-call(s32[2]{0:T(128)} %pad_add_fusion.1.at_ref.refs_0_, bf16[2048,384]{1,0:T(8,128)(2,1)} %copy-done.13, bf16[2048,384]{1,0:T(8,128)(2,1)} %copy-done.14, bf16[5376,1024]{1,0:T(8,128)(2,1)} %wq_ref.1, bf16[5376,512]{1,0:T(8,128)(2,1)} %wk_ref.1, ...), custom_call_target="tpu_custom_call" | custom-call | flops 112742891520 | tf_op jit(solution)/shard_map/input_last/pallas_call | solution.py:601
  244.7 11.2 %weight_terms.9 = bf16[1344,768]{1,0:T(8,128)(2,1)} custom-call(s32[2]{0:T(128)} %pad_add_fusion.1.at_ref.refs_0_, bf16[1344,512]{1,0:T(8,128)(2,1)} %copy-done.7, bf16[1344,256]{1,0:T(8,128)(2,1)} %copy-done.15, bf16[1344,256]{1,0:T(8,128)(2,1)} %copy-done.18, bf16[1344,256]{1,0:T(8,128)(2,1)} %copy-done.16, bf16[1344,256]{1,0:T(8,128)(2,1)} %copy-done.19, ...), custom_call_target="tpu_custom_call" | custom-call | flops 84557168640 | bytes 16220160 | tf_op jit(solution)/shard_map/weight_terms/pallas_call | solution.py:439
  257.9 5.5 %add_convert_fusion = bf16[256,5376]{1,0:T(8,128)(2,1)} fusion(f32[256,5376]{1,0:T(8,128)} %get-tuple-element.176, bf16[256,5376]{1,0:T(8,128)(2,1)} %collective-permute-done.24), kind=kLoop, calls=%fused_computation | loop fusion | flops 4128768 | bytes 11010048 | tf_op jit(solution)/shard_map/convert_element_type | solution.py:778
  263.3 2.7 assemble.1
  266.1 36.4 %reduce-scatter.14.cloned.1.call-done.part_ref = bf16[336,768]{1,0:T(8,128)(2,1)} async-done(((bf16[1344,768]{1,0:T(8,128)(2,1)}), bf16[336,768]{1,0:T(8,128)(2,1)}) %reduce-scatter.14.cloned.1.call-update) | async-done | bytes 516112 | tf_op jit(solution)/shard_map/reduce_scatter | solution.py:729
  (116 shorter events, 36.7 us)
Async XLA Ops:
  7.2 114.9 %reduce-scatter.6.cloned.1.call-start = ((), (), s32[]{:S(2)}) async-start(), calls=%async_computation.5 | async-start | bytes 860160 | tf_op jit(solution)/shard_map/reduce_scatter | solution.py:729
  12.2 26.3 %collective-permute-start = (bf16[528,512]{1,0:T(8,128)(2,1)}, bf16[528,512]{1,0:T(8,128)(2,1)S(1)}, u32[]{:S(2)}, u32[]{:S(2)}) collective-permute-start(bf16[528,512]{1,0:T(8,128)(2,1)} %get-tuple-element.107), channel_id=1, source_target_pairs={{0,2},{2,0},{4,6},{6,4},{1,3},{3,1},{5,7},{7,5},{8,10},{10,8},{12,... | collective-permute-start | bytes 1622024 | tf_op jit(solution)/shard_map/ppermute | solution.py:625
  15.1 25.5 %collective-permute-start.1 = (bf16[528,512]{1,0:T(8,128)(2,1)}, bf16[528,512]{1,0:T(8,128)(2,1)S(1)}, u32[]{:S(2)}, u32[]{:S(2)}) collective-permute-start(bf16[528,512]{1,0:T(8,128)(2,1)} %get-tuple-element.108), channel_id=1, source_target_pairs={{0,4},{2,6},{4,0},{6,2},{1,5},{3,7},{5,1},{7,3},{8,12},{10,14},{12... | collective-permute-start | bytes 1622024 | tf_op jit(solution)/shard_map/ppermute | solution.py:625
  16.6 24.0 %collective-permute-start.2 = (bf16[528,512]{1,0:T(8,128)(2,1)}, bf16[528,512]{1,0:T(8,128)(2,1)S(1)}, u32[]{:S(2)}, u32[]{:S(2)}) collective-permute-start(bf16[528,512]{1,0:T(8,128)(2,1)} %get-tuple-element.109), channel_id=1, source_target_pairs={{0,6},{2,4},{4,2},{6,0},{1,7},{3,5},{5,3},{7,1},{8,14},{10,12},{12... | collective-permute-start | bytes 1622024 | tf_op jit(solution)/shard_map/ppermute | solution.py:625
  40.7 10.1 %collective-permute-start.3 = (bf16[512,256]{1,0:T(8,128)(2,1)S(1)}, bf16[512,256]{1,0:T(8,128)(2,1)S(1)}, u32[]{:S(2)}, u32[]{:S(2)}) collective-permute-start(bf16[512,256]{1,0:T(8,128)(2,1)S(1)} %get-tuple-element.129), channel_id=1, source_target_pairs={{0,2},{2,0},{4,6},{6,4},{1,3},{3,1},{5,7},{7,5},{8,10},{10,8},{12,... | collective-permute-start | bytes 786440 | tf_op jit(solution)/shard_map/ppermute | solution.py:625
  42.0 14.1 %collective-permute-start.4 = (bf16[512,256]{1,0:T(8,128)(2,1)S(1)}, bf16[512,256]{1,0:T(8,128)(2,1)S(1)}, u32[]{:S(2)}, u32[]{:S(2)}) collective-permute-start(bf16[512,256]{1,0:T(8,128)(2,1)S(1)} %get-tuple-element.130), channel_id=1, source_target_pairs={{0,4},{2,6},{4,0},{6,2},{1,5},{3,7},{5,1},{7,3},{8,12},{10,14},{12... | collective-permute-start | bytes 786440 | tf_op jit(solution)/shard_map/ppermute | solution.py:625
  42.8 13.8 %collective-permute-start.5 = (bf16[512,256]{1,0:T(8,128)(2,1)S(1)}, bf16[512,256]{1,0:T(8,128)(2,1)S(1)}, u32[]{:S(2)}, u32[]{:S(2)}) collective-permute-start(bf16[512,256]{1,0:T(8,128)(2,1)S(1)} %get-tuple-element.131), channel_id=1, source_target_pairs={{0,6},{2,4},{4,2},{6,0},{1,7},{3,5},{5,3},{7,1},{8,14},{10,12},{12... | collective-permute-start | bytes 786440 | tf_op jit(solution)/shard_map/ppermute | solution.py:625
  44.2 33.0 %collective-permute-start.6 = (bf16[1344,256]{1,0:T(8,128)(2,1)S(1)}, bf16[1344,256]{1,0:T(8,128)(2,1)S(1)}, u32[]{:S(2)}, u32[]{:S(2)}) collective-permute-start(bf16[1344,256]{1,0:T(8,128)(2,1)S(1)} %get-tuple-element.134), channel_id=1, source_target_pairs={{0,2},{2,0},{4,6},{6,4},{1,3},{3,1},{5,7},{7,5},{8,10},{10,8},{12,... | collective-permute-start | bytes 2064392 | tf_op jit(solution)/shard_map/ppermute | solution.py:625
  45.5 38.5 %collective-permute-start.7 = (bf16[1344,256]{1,0:T(8,128)(2,1)S(1)}, bf16[1344,256]{1,0:T(8,128)(2,1)S(1)}, u32[]{:S(2)}, u32[]{:S(2)}) collective-permute-start(bf16[1344,256]{1,0:T(8,128)(2,1)S(1)} %get-tuple-element.135), channel_id=1, source_target_pairs={{0,4},{2,6},{4,0},{6,2},{1,5},{3,7},{5,1},{7,3},{8,12},{10,14},{12... | collective-permute-start | bytes 2064392 | tf_op jit(solution)/shard_map/ppermute | solution.py:625
  50.8 33.2 %collective-permute-start.8 = (bf16[1344,256]{1,0:T(8,128)(2,1)S(1)}, bf16[1344,256]{1,0:T(8,128)(2,1)S(1)}, u32[]{:S(2)}, u32[]{:S(2)}) collective-permute-start(bf16[1344,256]{1,0:T(8,128)(2,1)S(1)} %get-tuple-element.136), channel_id=1, source_target_pairs={{0,6},{2,4},{4,2},{6,0},{1,7},{3,5},{5,3},{7,1},{8,14},{10,12},{12... | collective-permute-start | bytes 2064392 | tf_op jit(solution)/shard_map/ppermute | solution.py:625
  84.6 18.6 %collective-permute-start.12 = (bf16[1344,256]{1,0:T(8,128)(2,1)}, bf16[1344,256]{1,0:T(8,128)(2,1)}, u32[]{:S(2)}, u32[]{:S(2)}) collective-permute-start(bf16[1344,256]{1,0:T(8,128)(2,1)} %get-tuple-element.145), channel_id=1, source_target_pairs={{0,2},{2,0},{4,6},{6,4},{1,3},{3,1},{5,7},{7,5},{8,10},{10,8},{12,... | collective-permute-start | bytes 2064392 | tf_op jit(solution)/shard_map/ppermute | solution.py:625
  85.2 18.1 %collective-permute-start.13 = (bf16[1344,256]{1,0:T(8,128)(2,1)S(1)}, bf16[1344,256]{1,0:T(8,128)(2,1)}, u32[]{:S(2)}, u32[]{:S(2)}) collective-permute-start(bf16[1344,256]{1,0:T(8,128)(2,1)S(1)} %get-tuple-element.146), channel_id=1, source_target_pairs={{0,4},{2,6},{4,0},{6,2},{1,5},{3,7},{5,1},{7,3},{8,12},{10,14},{12... | collective-permute-start | bytes 2064392 | tf_op jit(solution)/shard_map/ppermute | solution.py:625
  86.3 31.3 %collective-permute-start.14 = (bf16[1344,256]{1,0:T(8,128)(2,1)S(1)}, bf16[1344,256]{1,0:T(8,128)(2,1)}, u32[]{:S(2)}, u32[]{:S(2)}) collective-permute-start(bf16[1344,256]{1,0:T(8,128)(2,1)S(1)} %get-tuple-element.147), channel_id=1, source_target_pairs={{0,6},{2,4},{4,2},{6,0},{1,7},{3,5},{5,3},{7,1},{8,14},{10,12},{12... | collective-permute-start | bytes 2064392 | tf_op jit(solution)/shard_map/ppermute | solution.py:625
  96.0 130.3 %reduce-scatter.8.cloned.1.call-start = ((), (), s32[]{:S(2)}) async-start(), calls=%async_computation.6 | async-start | bytes 1720320 | tf_op jit(solution)/shard_map/reduce_scatter | solution.py:729
  118.1 37.0 %collective-permute-start.18 = (bf16[2048,384]{1,0:T(8,128)(2,1)}, bf16[2048,384]{1,0:T(8,128)(2,1)S(1)}, u32[]{:S(2)}, u32[]{:S(2)}) collective-permute-start(bf16[2048,384]{1,0:T(8,128)(2,1)} %get-tuple-element.163.refs_7_.refs_0_), channel_id=1, source_target_pairs={{0,2},{2,0},{4,6},{6,4},{1,3},{3,1},{5,7},{7,5},{8,10},{10,8},{12,... | collective-permute-start | bytes 4718600 | tf_op jit(solution)/shard_map/ppermute | solution.py:625
  119.5 36.7 %collective-permute-start.19 = (bf16[2048,384]{1,0:T(8,128)(2,1)}, bf16[2048,384]{1,0:T(8,128)(2,1)S(1)}, u32[]{:S(2)}, u32[]{:S(2)}) collective-permute-start(bf16[2048,384]{1,0:T(8,128)(2,1)} %get-tuple-element.164.refs_8_.refs_3_), channel_id=1, source_target_pairs={{0,4},{2,6},{4,0},{6,2},{1,5},{3,7},{5,1},{7,3},{8,12},{10,14},{12... | collective-permute-start | bytes 4718600 | tf_op jit(solution)/shard_map/ppermute | solution.py:625
  131.4 124.6 %reduce-scatter.10.cloned.1.call-start = ((), (), s32[]{:S(2)}) async-start(), calls=%async_computation.7 | async-start | bytes 2580480 | tf_op jit(solution)/shard_map/reduce_scatter | solution.py:729
  156.3 36.1 %collective-permute-start.20 = (bf16[2048,384]{1,0:T(8,128)(2,1)}, bf16[2048,384]{1,0:T(8,128)(2,1)}, u32[]{:S(2)}, u32[]{:S(2)}) collective-permute-start(bf16[2048,384]{1,0:T(8,128)(2,1)} %get-tuple-element.163.refs_7_.refs_0_), channel_id=1, source_target_pairs={{0,4},{2,6},{4,0},{6,2},{1,5},{3,7},{5,1},{7,3},{8,12},{10,14},{12... | collective-permute-start | bytes 4718600 | tf_op jit(solution)/shard_map/ppermute | solution.py:625
  156.8 35.9 %collective-permute-start.21 = (bf16[2048,384]{1,0:T(8,128)(2,1)}, bf16[2048,384]{1,0:T(8,128)(2,1)}, u32[]{:S(2)}, u32[]{:S(2)}) collective-permute-start(bf16[2048,384]{1,0:T(8,128)(2,1)} %get-tuple-element.164.refs_8_.refs_3_), channel_id=1, source_target_pairs={{0,2},{2,0},{4,6},{6,4},{1,3},{3,1},{5,7},{7,5},{8,10},{10,8},{12,... | collective-permute-start | bytes 4718600 | tf_op jit(solution)/shard_map/ppermute | solution.py:625
  169.4 88.4 %reduce-scatter.12.cloned.1.call-start = ((), (), s32[]{:S(2)}) async-start(), calls=%async_computation.8 | async-start | bytes 2580480 | tf_op jit(solution)/shard_map/reduce_scatter | solution.py:729
  192.7 34.9 %collective-permute-start.22 = (bf16[2048,384]{1,0:T(8,128)(2,1)}, bf16[2048,384]{1,0:T(8,128)(2,1)S(1)}, u32[]{:S(2)}, u32[]{:S(2)}) collective-permute-start(bf16[2048,384]{1,0:T(8,128)(2,1)} %copy-done.10), channel_id=1, source_target_pairs={{0,4},{2,6},{4,0},{6,2},{1,5},{3,7},{5,1},{7,3},{8,12},{10,14},{12... | collective-permute-start | bytes 4718600 | tf_op jit(solution)/shard_map/ppermute | solution.py:625
  194.2 34.5 %collective-permute-start.23 = (bf16[2048,384]{1,0:T(8,128)(2,1)}, bf16[2048,384]{1,0:T(8,128)(2,1)S(1)}, u32[]{:S(2)}, u32[]{:S(2)}) collective-permute-start(bf16[2048,384]{1,0:T(8,128)(2,1)} %copy-done.11), channel_id=1, source_target_pairs={{0,2},{2,0},{4,6},{6,4},{1,3},{3,1},{5,7},{7,5},{8,10},{10,8},{12,... | collective-permute-start | bytes 4718600 | tf_op jit(solution)/shard_map/ppermute | solution.py:625
  206.0 96.5 %reduce-scatter.14.cloned.1.call-start = ((), (), s32[]{:S(2)}) async-start(), calls=%async_computation.9 | async-start | bytes 2580480 | tf_op jit(solution)/shard_map/reduce_scatter | solution.py:729
  244.7 13.1 %collective-permute-start.24 = (bf16[256,5376]{1,0:T(8,128)(2,1)}, bf16[256,5376]{1,0:T(8,128)(2,1)}, u32[]{:S(2)}, u32[]{:S(2)}) collective-permute-start(bf16[256,5376]{1,0:T(8,128)(2,1)} %get-tuple-element.175), channel_id=1, source_target_pairs={{0,1},{1,0},{2,3},{3,2},{4,5},{5,4},{6,7},{7,6},{8,9},{9,8},{10,11... | collective-permute-start | bytes 8257544 | tf_op jit(solution)/shard_map/ppermute | solution.py:625
  (27 other events, 130.1 us)
Sparse Core Ops, SparseCore 0:
  96.1 22.4 reduce-scatter.5
  131.5 32.4 reduce-scatter.7
  169.6 43.4 reduce-scatter.9
  215.4 42.4 reduce-scatter.11
  260.0 42.4 reduce-scatter.13

commit v2 on v1

--- a/solution.py
+++ b/solution.py
@@ -164,7 +164,8 @@
 
 TILE = 256
 EXTRA = 16
-RADIX = 128
+RADIX_BITS = 7
+RADIX = 1 << RADIX_BITS
 NEGATIVE = -1e30
 LOG2E = 1.4426950408889634
 VMEM_LIMIT = 48 * 1024 * 1024
@@ -203,32 +204,38 @@
     return pl.ds(pl.multiple_of(index * size, size), size)
 
 
-def pack_heads_kernel(blocks, wide, narrow, at_ref, q_ref, k_ref, v_ref, extra_ref, *outs):
+def pack_heads_kernel(blocks, wide, narrow, at_ref, q_ref, k_ref, v_ref, places_ref, *outs):
     me = at_ref[0]
     count = q_ref.shape[0]
+    places = jnp.broadcast_to(places_ref[...], (EXTRA, count))
+    row = lax.broadcasted_iota(jnp.int32, (EXTRA, count), 0)
+    digits = jnp.where(row == 0, places >> RADIX_BITS, jnp.where(row == 1, places & (RADIX - 1), 0))
+    digits = digits.astype(jnp.float32).astype(jnp.bfloat16)
     for part in range(blocks):
         there = me ^ part
         out = outs[part]
         out[:count, :wide] = q_ref[:, aligned(there, wide)]
         out[:count, wide : wide + narrow] = k_ref[:, aligned(there, narrow)]
         out[:count, wide + narrow :] = v_ref[:, aligned(there, narrow)]
-        out[count:, :] = extra_ref[...]
-
-
-def pack_heads(at, queries, key_states, value_states, extra, blocks, wide, narrow):
+        out[count:, :count] = digits
+        if out.shape[1] > count:
+            out[count:, count:] = jnp.zeros((EXTRA, out.shape[1] - count), out.dtype)
+
+
+def pack_heads(at, queries, key_states, value_states, places, blocks, wide, narrow):
     count = queries.shape[0]
     shape = jax.ShapeDtypeStruct((count + EXTRA, wide + 2 * narrow), queries.dtype)
     return pl.pallas_call(
         functools.partial(pack_heads_kernel, blocks, wide, narrow),
         out_shape=(shape,) * blocks,
-        in_specs=[scalars()] + [pl.BlockSpec(x.shape, lambda: (0, 0)) for x in (queries, key_states, value_states, extra)],
+        in_specs=[scalars()] + [pl.BlockSpec(x.shape, lambda: (0, 0)) for x in (queries, key_states, value_states, places)],
         out_specs=(whole(),) * blocks,
         compiler_params=params(VMEM_MOST),
         cost_estimate=pl.CostEstimate(
             flops=0, bytes_accessed=4 * blocks * count * (wide + 2 * narrow), transcendentals=0
         ),
         name="pack_heads",
-    )(at, queries, key_states, value_states, extra)
+    )(at, queries, key_states, value_states, places)
 
 
 def pack_rows_kernel(blocks, replicas, rows, at_ref, x_ref, own_ref, *rest):
@@ -508,14 +515,14 @@
     return pl.pallas_call(
         functools.partial(assemble_last_kernel, places),
         out_shape=tuple(jax.ShapeDtypeStruct(x.shape, x.dtype) for x in grads),
-        in_specs=[scalars(), whole()] + [anywhere] * 4,
+        in_specs=[scalars(), pl.BlockSpec(part.shape, lambda: (0, 0))] + [anywhere] * 4,
         out_specs=(anywhere,) * 4,
         scratch_shapes=[
             pltpu.VMEM(part.shape, jnp.float32),
             pltpu.SemaphoreType.DMA((len(places),)),
         ],
         input_output_aliases={2: 0, 3: 1, 4: 2, 5: 3},
-        compiler_params=params(),
+        compiler_params=params(VMEM_MOST),
         name="assemble_last",
     )(at, part, *grads)
 
@@ -681,10 +688,8 @@
 
     barrier = lax.optimization_barrier
 
-    digits = jnp.stack([positions // RADIX, positions % RADIX]).astype(jnp.bfloat16)
-    extra = jnp.pad(digits, ((0, EXTRA - 2), (0, wide + 2 * narrow - count)))
     packs = list(
-        pack_heads(at, queries, key_states, value_states, extra, blocks, wide, narrow)
+        pack_heads(at, queries, key_states, value_states, positions[None, :], blocks, wide, narrow)
     )
     after, packs = barrier((out_grad, packs))
     for part in range(1, blocks):

time: 313 us -> 311 us (level)
  no operation moved by 1% of the time
where the time goes in v2:
time: 311 us; the launch traced here: 310 us
  waiting for transfers between devices  126 us (41%)
  Pallas kernels  123 us (40%)
  starting transfers between devices  22.5 us (7%)
  between operations  14.1 us (5%)
  other arithmetic  10.6 us (3%)
  matrix products  10.2 us (3%)
  local copies, waits for them, and re-layouts  3.47 us (1%)
    ppermute x25, waiting for transfers between devices, swap(): return lax.ppermute(x, axis, [(i, i ^ by) for i in range(count)])  87.3 us
    pallas_call x5, Pallas kernels, weight_terms(): pl.pallas_call(functools.partial(weight_terms_kernel, blocks, jobs), out_...  49.5 us
    reduce_scatter x5, waiting for transfers between devices, summed(): return lax.psum_scatter(term, 'dp', scatter_dimension=0, tiled=True)  38.4 us
    ppermute x25, starting transfers between devices, swap(): return lax.ppermute(x, axis, [(i, i ^ by) for i in range(count)])  22.3 us
    pallas_call x1, Pallas kernels, attention(): pl.pallas_call(functools.partial(attention_kernel, blocks, count, heads,...  20.7 us
    pallas_call x1, Pallas kernels, input_first(): pl.pallas_call(functools.partial(input_first_kernel, blocks, wide, narrow...  20.1 us
    pallas_call x1, Pallas kernels, input_last(): pl.pallas_call(functools.partial(input_last_kernel, wide), out_shape=(jax...  14.9 us
    pallas_call x2, Pallas kernels, pack_rows(): pl.pallas_call(functools.partial(pack_rows_kernel, blocks, replicas, rows...  10.2 us
  transfers between devices with their start and end apart: 30, of which 17 were waited for; matrix products, arithmetic and copies ran while one was open for 7% of the time, Pallas kernels for 38%

profile of v2, /device:TPU:0, one launch (start us, length us, event | category | flops | bytes accessed | tf_op | source)
XLA Modules:
  0.0 310.2 jit_solution(16794846469042495073)
XLA Ops:
  7.9 3.2 %pack_heads.1 = (bf16[528,512]{1,0:T(8,128)(2,1)}, bf16[528,512]{1,0:T(8,128)(2,1)}, bf16[528,512]{1,0:T(8,128)(2,1)}, bf16[528,512]{1,0:T(8,128)(2,1)}) custom-call(s32[2]{0:T(128)} %pad_add_fusion.1.at_ref.refs_0_, bf16[512,1024]{1,0:T(8,128)(2,1)} %q_ref.1, bf16[512,512]{1,0:T(8,128)(2,1)} %k_ref.1, bf16[512,512]{1,0:T(8,128)(2,1)} %v_ref.1, ...), custom_call_target="tpu_custom_call" | custom-call | bytes 4194304 | tf_op jit(solution)/shard_map/pack_heads/pallas_call | solution.py:228
  11.1 2.9 collective-permute-start
  15.5 10.2 %convolution_convert_fusion = bf16[512,1024]{1,0:T(8,128)(2,1)S(1)} fusion(bf16[512,5376]{1,0:T(8,128)(2,1)} %x_ref.2, bf16[5376,1024]{1,0:T(8,128)(2,1)} %param.19), kind=kOutput, calls=%fused_computation.3 | convolution fusion | flops 5637668864 | bytes 17563648 | tf_op jit(solution)/shard_map/dot_general | solution.py:697
  25.9 4.6 %pack_rows.2 = (bf16[1344,512]{1,0:T(8,128)(2,1)S(1)}, bf16[1344,256]{1,0:T(8,128)(2,1)S(1)}, bf16[1344,256]{1,0:T(8,128)(2,1)S(1)}, bf16[1344,256]{1,0:T(8,128)(2,1)S(1)}) custom-call(s32[2]{0:T(128)S(1)} %copy-done.4, bf16[512,5376]{1,0:T(8,128)(2,1)} %x_ref.2), custom_call_target="tpu_custom_call" | custom-call | bytes 16515072 | tf_op jit(solution)/shard_map/pack_rows/pallas_call | solution.py:269
  31.6 5.6 %pack_rows.3 = (bf16[1344,512]{1,0:T(8,128)(2,1)S(1)}, bf16[1344,256]{1,0:T(8,128)(2,1)}, bf16[1344,256]{1,0:T(8,128)(2,1)S(1)}, bf16[1344,256]{1,0:T(8,128)(2,1)S(1)}) custom-call(s32[2]{0:T(128)S(1)} %copy-done.4, bf16[512,5376]{1,0:T(8,128)(2,1)} %x_ref.3), custom_call_target="tpu_custom_call" | custom-call | bytes 16515072 | tf_op jit(solution)/shard_map/pack_rows/pallas_call | solution.py:269
  37.3 2.2 collective-permute-done.1.refs_3_
  45.2 3.7 %multiply_sine_fusion = (f32[2048,64]{1,0:T(8,128)S(1)}, f32[2048,64]{1,0:T(8,128)S(1)}, f32[2048,64]{1,0:T(8,128)S(1)}) fusion(f32[64]{0:T(128)S(1)} %multiply_power_fusion, f32[2048]{0:T(1024)S(1)} %add_convert_fusion.1), kind=kLoop, calls=%fused_computation.1 | loop fusion | flops 262144 | bytes 1581312 | tf_op jit(solution)/shard_map/sin | solution.py:641
  51.1 3.8 %collective-permute-done.4.refs_7_ = bf16[512,256]{1,0:T(8,128)(2,1)S(1)} collective-permute-done((bf16[512,256]{1,0:T(8,128)(2,1)S(1)}, bf16[512,256]{1,0:T(8,128)(2,1)S(1)}, u32[]{:S(2)}, u32[]{:S(2)}) %collective-permute-start.4) | collective-permute-done | bytes 262176 | tf_op jit(solution)/shard_map/ppermute | solution.py:632
  55.4 20.7 %attention_backward.1 = (bf16[2048,384]{1,0:T(8,128)(2,1)}, bf16[2048,384]{1,0:T(8,128)(2,1)}) custom-call(s32[2]{0:T(128)S(1)} %copy-done.4, bf16[528,512]{1,0:T(8,128)(2,1)S(1)} %copy-done.8, bf16[528,512]{1,0:T(8,128)(2,1)S(1)} %collective-permute-done.refs_2_, bf16[528,512]{1,0:T(8,128)(2,1)S(1)} %collective-permute-done.1.refs_3_, ...), custom_call_target="tpu_custom_call" | custom-call | flops 6710886400 | bytes 6291456 | tf_op jit(solution)/shard_map/attention_backward/pallas_call | solution.py:384
  76.1 6.7 %collective-permute-done.7.refs_3_ = bf16[1344,256]{1,0:T(8,128)(2,1)S(1)} collective-permute-done((bf16[1344,256]{1,0:T(8,128)(2,1)S(1)}, bf16[1344,256]{1,0:T(8,128)(2,1)S(1)}, u32[]{:S(2)}, u32[]{:S(2)}) %collective-permute-start.7) | collective-permute-done | bytes 688160 | tf_op jit(solution)/shard_map/ppermute | solution.py:632
  88.1 6.7 %weight_terms.5 = bf16[1344,256]{1,0:T(8,128)(2,1)} custom-call(s32[2]{0:T(128)} %pad_add_fusion.1.at_ref.refs_0_, bf16[1344,512]{1,0:T(8,128)(2,1)} %copy-done.6, bf16[1344,256]{1,0:T(8,128)(2,1)} %copy-done.14, bf16[1344,256]{1,0:T(8,128)(2,1)} %copy-done.17, bf16[1344,256]{1,0:T(8,128)(2,1)} %copy-done.15, bf16[1344,256]{1,0:T(8,128)(2,1)} %copy-done.18, ...), custom_call_target="tpu_custom_call" | custom-call | flops 8455716864 | bytes 7241728 | tf_op jit(solution)/shard_map/weight_terms/pallas_call | solution.py:446
  94.8 7.2 %collective-permute-done.12.refs_1_.refs_8_ = bf16[1344,256]{1,0:T(8,128)(2,1)} collective-permute-done((bf16[1344,256]{1,0:T(8,128)(2,1)}, bf16[1344,256]{1,0:T(8,128)(2,1)}, u32[]{:S(2)}, u32[]{:S(2)}) %collective-permute-start.12) | collective-permute-done | bytes 688160 | tf_op jit(solution)/shard_map/ppermute | solution.py:632
  102.2 14.3 %collective-permute-done.14.refs_5_.refs_12_ = bf16[1344,256]{1,0:T(8,128)(2,1)} collective-permute-done((bf16[1344,256]{1,0:T(8,128)(2,1)S(1)}, bf16[1344,256]{1,0:T(8,128)(2,1)}, u32[]{:S(2)}, u32[]{:S(2)}) %collective-permute-start.14) | collective-permute-done | bytes 688160 | tf_op jit(solution)/shard_map/ppermute | solution.py:632
  120.9 9.3 %weight_terms.6 = bf16[1344,512]{1,0:T(8,128)(2,1)} custom-call(s32[2]{0:T(128)} %pad_add_fusion.1.at_ref.refs_0_, bf16[1344,512]{1,0:T(8,128)(2,1)} %copy-done.7, bf16[1344,256]{1,0:T(8,128)(2,1)} %collective-permute-done.12.refs_1_.refs_8_, bf16[1344,256]{1,0:T(8,128)(2,1)} %collective-permute-done.15.refs_2_.refs_9_, ...), custom_call_target="tpu_custom_call" | custom-call | flops 16911433728 | bytes 8978432 | tf_op jit(solution)/shard_map/weight_terms/pallas_call | solution.py:446
  130.3 23.7 %collective-permute-done.18.refs_14_.refs_1_ = bf16[2048,384]{1,0:T(8,128)(2,1)S(1)} collective-permute-done((bf16[2048,384]{1,0:T(8,128)(2,1)}, bf16[2048,384]{1,0:T(8,128)(2,1)S(1)}, u32[]{:S(2)}, u32[]{:S(2)}) %collective-permute-start.18) | collective-permute-done | bytes 1572896 | tf_op jit(solution)/shard_map/ppermute | solution.py:632
  157.1 11.2 %weight_terms.7 = bf16[1344,768]{1,0:T(8,128)(2,1)} custom-call(s32[2]{0:T(128)} %pad_add_fusion.1.at_ref.refs_0_, bf16[1344,512]{1,0:T(8,128)(2,1)} %copy-done.6, bf16[1344,256]{1,0:T(8,128)(2,1)} %copy-done.14, bf16[1344,256]{1,0:T(8,128)(2,1)} %copy-done.17, bf16[1344,256]{1,0:T(8,128)(2,1)} %copy-done.15, bf16[1344,256]{1,0:T(8,128)(2,1)} %copy-done.18, ...), custom_call_target="tpu_custom_call" | custom-call | flops 84557168640 | bytes 16220160 | tf_op jit(solution)/shard_map/weight_terms/pallas_call | solution.py:446
  168.3 22.9 %collective-permute-done.20.refs_14_.refs_2_ = bf16[2048,384]{1,0:T(8,128)(2,1)} collective-permute-done((bf16[2048,384]{1,0:T(8,128)(2,1)}, bf16[2048,384]{1,0:T(8,128)(2,1)}, u32[]{:S(2)}, u32[]{:S(2)}) %collective-permute-start.20) | collective-permute-done | bytes 1572896 | tf_op jit(solution)/shard_map/ppermute | solution.py:632
  193.7 11.2 %weight_terms.8 = bf16[1344,768]{1,0:T(8,128)(2,1)} custom-call(s32[2]{0:T(128)} %pad_add_fusion.1.at_ref.refs_0_, bf16[1344,512]{1,0:T(8,128)(2,1)} %copy-done.6, bf16[1344,256]{1,0:T(8,128)(2,1)} %copy-done.14, bf16[1344,256]{1,0:T(8,128)(2,1)} %copy-done.17, bf16[1344,256]{1,0:T(8,128)(2,1)} %copy-done.15, bf16[1344,256]{1,0:T(8,128)(2,1)} %copy-done.18, ...), custom_call_target="tpu_custom_call" | custom-call | flops 84557168640 | bytes 16220160 | tf_op jit(solution)/shard_map/weight_terms/pallas_call | solution.py:446
  204.9 20.1 %input_first.1.part_ref = f32[512,5376]{1,0:T(8,128)} custom-call(s32[2]{0:T(128)} %pad_add_fusion.1.at_ref.refs_0_, bf16[2048,384]{1,0:T(8,128)(2,1)} %get-tuple-element.163.refs_7_.refs_0_, bf16[2048,384]{1,0:T(8,128)(2,1)} %copy-done.9, bf16[2048,384]{1,0:T(8,128)(2,1)} %collective-permute-done.20.refs_14_.refs_2_, ...), custom_call_target="tpu_custom_call" | custom-call | flops 5637144576 | tf_op jit(solution)/shard_map/input_first/pallas_call | solution.py:571
  228.7 14.9 %input_last.1 = (f32[256,5376]{1,0:T(8,128)}, bf16[256,5376]{1,0:T(8,128)(2,1)}) custom-call(s32[2]{0:T(128)} %pad_add_fusion.1.at_ref.refs_0_, bf16[2048,384]{1,0:T(8,128)(2,1)} %copy-done.12, bf16[2048,384]{1,0:T(8,128)(2,1)} %copy-done.13, bf16[5376,1024]{1,0:T(8,128)(2,1)} %wq_ref.1, bf16[5376,512]{1,0:T(8,128)(2,1)} %wk_ref.1, ...), custom_call_target="tpu_custom_call" | custom-call | flops 112742891520 | tf_op jit(solution)/shard_map/input_last/pallas_call | solution.py:608
  243.6 11.2 %weight_terms.9 = bf16[1344,768]{1,0:T(8,128)(2,1)} custom-call(s32[2]{0:T(128)} %pad_add_fusion.1.at_ref.refs_0_, bf16[1344,512]{1,0:T(8,128)(2,1)} %copy-done.6, bf16[1344,256]{1,0:T(8,128)(2,1)} %copy-done.14, bf16[1344,256]{1,0:T(8,128)(2,1)} %copy-done.17, bf16[1344,256]{1,0:T(8,128)(2,1)} %copy-done.15, bf16[1344,256]{1,0:T(8,128)(2,1)} %copy-done.18, ...), custom_call_target="tpu_custom_call" | custom-call | flops 84557168640 | bytes 16220160 | tf_op jit(solution)/shard_map/weight_terms/pallas_call | solution.py:446
  256.6 5.5 %add_convert_fusion = bf16[256,5376]{1,0:T(8,128)(2,1)} fusion(f32[256,5376]{1,0:T(8,128)} %get-tuple-element.176, bf16[256,5376]{1,0:T(8,128)(2,1)} %collective-permute-done.24), kind=kLoop, calls=%fused_computation | loop fusion | flops 4128768 | bytes 11010048 | tf_op jit(solution)/shard_map/convert_element_type | solution.py:783
  262.1 2.7 assemble.1
  264.8 36.7 %reduce-scatter.14.cloned.1.call-done.part_ref = bf16[336,768]{1,0:T(8,128)(2,1)} async-done(((bf16[1344,768]{1,0:T(8,128)(2,1)}), bf16[336,768]{1,0:T(8,128)(2,1)}) %reduce-scatter.14.cloned.1.call-update) | async-done | bytes 516112 | tf_op jit(solution)/shard_map/reduce_scatter | solution.py:734
  (110 shorter events, 34.9 us)
Async XLA Ops:
  7.2 113.7 %reduce-scatter.6.cloned.1.call-start = ((), (), s32[]{:S(2)}) async-start(), calls=%async_computation.5 | async-start | bytes 860160 | tf_op jit(solution)/shard_map/reduce_scatter | solution.py:734
  11.1 26.3 %collective-permute-start = (bf16[528,512]{1,0:T(8,128)(2,1)}, bf16[528,512]{1,0:T(8,128)(2,1)S(1)}, u32[]{:S(2)}, u32[]{:S(2)}) collective-permute-start(bf16[528,512]{1,0:T(8,128)(2,1)} %get-tuple-element.107), channel_id=1, source_target_pairs={{0,2},{2,0},{4,6},{6,4},{1,3},{3,1},{5,7},{7,5},{8,10},{10,8},{12,... | collective-permute-start | bytes 1622024 | tf_op jit(solution)/shard_map/ppermute | solution.py:632
  14.0 25.5 %collective-permute-start.1 = (bf16[528,512]{1,0:T(8,128)(2,1)}, bf16[528,512]{1,0:T(8,128)(2,1)S(1)}, u32[]{:S(2)}, u32[]{:S(2)}) collective-permute-start(bf16[528,512]{1,0:T(8,128)(2,1)} %get-tuple-element.108), channel_id=1, source_target_pairs={{0,4},{2,6},{4,0},{6,2},{1,5},{3,7},{5,1},{7,3},{8,12},{10,14},{12... | collective-permute-start | bytes 1622024 | tf_op jit(solution)/shard_map/ppermute | solution.py:632
  15.5 24.0 %collective-permute-start.2 = (bf16[528,512]{1,0:T(8,128)(2,1)}, bf16[528,512]{1,0:T(8,128)(2,1)S(1)}, u32[]{:S(2)}, u32[]{:S(2)}) collective-permute-start(bf16[528,512]{1,0:T(8,128)(2,1)} %get-tuple-element.109), channel_id=1, source_target_pairs={{0,6},{2,4},{4,2},{6,0},{1,7},{3,5},{5,3},{7,1},{8,14},{10,12},{12... | collective-permute-start | bytes 1622024 | tf_op jit(solution)/shard_map/ppermute | solution.py:632
  39.5 10.1 %collective-permute-start.3 = (bf16[512,256]{1,0:T(8,128)(2,1)S(1)}, bf16[512,256]{1,0:T(8,128)(2,1)S(1)}, u32[]{:S(2)}, u32[]{:S(2)}) collective-permute-start(bf16[512,256]{1,0:T(8,128)(2,1)S(1)} %get-tuple-element.129), channel_id=1, source_target_pairs={{0,2},{2,0},{4,6},{6,4},{1,3},{3,1},{5,7},{7,5},{8,10},{10,8},{12,... | collective-permute-start | bytes 786440 | tf_op jit(solution)/shard_map/ppermute | solution.py:632
  40.8 14.1 %collective-permute-start.4 = (bf16[512,256]{1,0:T(8,128)(2,1)S(1)}, bf16[512,256]{1,0:T(8,128)(2,1)S(1)}, u32[]{:S(2)}, u32[]{:S(2)}) collective-permute-start(bf16[512,256]{1,0:T(8,128)(2,1)S(1)} %get-tuple-element.130), channel_id=1, source_target_pairs={{0,4},{2,6},{4,0},{6,2},{1,5},{3,7},{5,1},{7,3},{8,12},{10,14},{12... | collective-permute-start | bytes 786440 | tf_op jit(solution)/shard_map/ppermute | solution.py:632
  41.7 13.8 %collective-permute-start.5 = (bf16[512,256]{1,0:T(8,128)(2,1)S(1)}, bf16[512,256]{1,0:T(8,128)(2,1)S(1)}, u32[]{:S(2)}, u32[]{:S(2)}) collective-permute-start(bf16[512,256]{1,0:T(8,128)(2,1)S(1)} %get-tuple-element.131), channel_id=1, source_target_pairs={{0,6},{2,4},{4,2},{6,0},{1,7},{3,5},{5,3},{7,1},{8,14},{10,12},{12... | collective-permute-start | bytes 786440 | tf_op jit(solution)/shard_map/ppermute | solution.py:632
  43.1 33.0 %collective-permute-start.6 = (bf16[1344,256]{1,0:T(8,128)(2,1)S(1)}, bf16[1344,256]{1,0:T(8,128)(2,1)S(1)}, u32[]{:S(2)}, u32[]{:S(2)}) collective-permute-start(bf16[1344,256]{1,0:T(8,128)(2,1)S(1)} %get-tuple-element.134), channel_id=1, source_target_pairs={{0,2},{2,0},{4,6},{6,4},{1,3},{3,1},{5,7},{7,5},{8,10},{10,8},{12,... | collective-permute-start | bytes 2064392 | tf_op jit(solution)/shard_map/ppermute | solution.py:632
  44.3 38.5 %collective-permute-start.7 = (bf16[1344,256]{1,0:T(8,128)(2,1)S(1)}, bf16[1344,256]{1,0:T(8,128)(2,1)S(1)}, u32[]{:S(2)}, u32[]{:S(2)}) collective-permute-start(bf16[1344,256]{1,0:T(8,128)(2,1)S(1)} %get-tuple-element.135), channel_id=1, source_target_pairs={{0,4},{2,6},{4,0},{6,2},{1,5},{3,7},{5,1},{7,3},{8,12},{10,14},{12... | collective-permute-start | bytes 2064392 | tf_op jit(solution)/shard_map/ppermute | solution.py:632
  49.6 33.2 %collective-permute-start.8 = (bf16[1344,256]{1,0:T(8,128)(2,1)S(1)}, bf16[1344,256]{1,0:T(8,128)(2,1)S(1)}, u32[]{:S(2)}, u32[]{:S(2)}) collective-permute-start(bf16[1344,256]{1,0:T(8,128)(2,1)S(1)} %get-tuple-element.136), channel_id=1, source_target_pairs={{0,6},{2,4},{4,2},{6,0},{1,7},{3,5},{5,3},{7,1},{8,14},{10,12},{12... | collective-permute-start | bytes 2064392 | tf_op jit(solution)/shard_map/ppermute | solution.py:632
  83.5 18.6 %collective-permute-start.12 = (bf16[1344,256]{1,0:T(8,128)(2,1)}, bf16[1344,256]{1,0:T(8,128)(2,1)}, u32[]{:S(2)}, u32[]{:S(2)}) collective-permute-start(bf16[1344,256]{1,0:T(8,128)(2,1)} %get-tuple-element.145), channel_id=1, source_target_pairs={{0,2},{2,0},{4,6},{6,4},{1,3},{3,1},{5,7},{7,5},{8,10},{10,8},{12,... | collective-permute-start | bytes 2064392 | tf_op jit(solution)/shard_map/ppermute | solution.py:632
  84.1 18.1 %collective-permute-start.13 = (bf16[1344,256]{1,0:T(8,128)(2,1)S(1)}, bf16[1344,256]{1,0:T(8,128)(2,1)}, u32[]{:S(2)}, u32[]{:S(2)}) collective-permute-start(bf16[1344,256]{1,0:T(8,128)(2,1)S(1)} %get-tuple-element.146), channel_id=1, source_target_pairs={{0,4},{2,6},{4,0},{6,2},{1,5},{3,7},{5,1},{7,3},{8,12},{10,14},{12... | collective-permute-start | bytes 2064392 | tf_op jit(solution)/shard_map/ppermute | solution.py:632
  85.2 31.3 %collective-permute-start.14 = (bf16[1344,256]{1,0:T(8,128)(2,1)S(1)}, bf16[1344,256]{1,0:T(8,128)(2,1)}, u32[]{:S(2)}, u32[]{:S(2)}) collective-permute-start(bf16[1344,256]{1,0:T(8,128)(2,1)S(1)} %get-tuple-element.147), channel_id=1, source_target_pairs={{0,6},{2,4},{4,2},{6,0},{1,7},{3,5},{5,3},{7,1},{8,14},{10,12},{12... | collective-permute-start | bytes 2064392 | tf_op jit(solution)/shard_map/ppermute | solution.py:632
  94.8 130.2 %reduce-scatter.8.cloned.1.call-start = ((), (), s32[]{:S(2)}) async-start(), calls=%async_computation.6 | async-start | bytes 1720320 | tf_op jit(solution)/shard_map/reduce_scatter | solution.py:734
  117.0 37.0 %collective-permute-start.18 = (bf16[2048,384]{1,0:T(8,128)(2,1)}, bf16[2048,384]{1,0:T(8,128)(2,1)S(1)}, u32[]{:S(2)}, u32[]{:S(2)}) collective-permute-start(bf16[2048,384]{1,0:T(8,128)(2,1)} %get-tuple-element.163.refs_7_.refs_0_), channel_id=1, source_target_pairs={{0,2},{2,0},{4,6},{6,4},{1,3},{3,1},{5,7},{7,5},{8,10},{10,8},{12,... | collective-permute-start | bytes 4718600 | tf_op jit(solution)/shard_map/ppermute | solution.py:632
  118.4 36.7 %collective-permute-start.19 = (bf16[2048,384]{1,0:T(8,128)(2,1)}, bf16[2048,384]{1,0:T(8,128)(2,1)S(1)}, u32[]{:S(2)}, u32[]{:S(2)}) collective-permute-start(bf16[2048,384]{1,0:T(8,128)(2,1)} %get-tuple-element.164.refs_8_.refs_3_), channel_id=1, source_target_pairs={{0,4},{2,6},{4,0},{6,2},{1,5},{3,7},{5,1},{7,3},{8,12},{10,14},{12... | collective-permute-start | bytes 4718600 | tf_op jit(solution)/shard_map/ppermute | solution.py:632
  130.2 124.6 %reduce-scatter.10.cloned.1.call-start = ((), (), s32[]{:S(2)}) async-start(), calls=%async_computation.7 | async-start | bytes 2580480 | tf_op jit(solution)/shard_map/reduce_scatter | solution.py:734
  155.1 36.1 %collective-permute-start.20 = (bf16[2048,384]{1,0:T(8,128)(2,1)}, bf16[2048,384]{1,0:T(8,128)(2,1)}, u32[]{:S(2)}, u32[]{:S(2)}) collective-permute-start(bf16[2048,384]{1,0:T(8,128)(2,1)} %get-tuple-element.163.refs_7_.refs_0_), channel_id=1, source_target_pairs={{0,4},{2,6},{4,0},{6,2},{1,5},{3,7},{5,1},{7,3},{8,12},{10,14},{12... | collective-permute-start | bytes 4718600 | tf_op jit(solution)/shard_map/ppermute | solution.py:632
  155.7 35.9 %collective-permute-start.21 = (bf16[2048,384]{1,0:T(8,128)(2,1)}, bf16[2048,384]{1,0:T(8,128)(2,1)}, u32[]{:S(2)}, u32[]{:S(2)}) collective-permute-start(bf16[2048,384]{1,0:T(8,128)(2,1)} %get-tuple-element.164.refs_8_.refs_3_), channel_id=1, source_target_pairs={{0,2},{2,0},{4,6},{6,4},{1,3},{3,1},{5,7},{7,5},{8,10},{10,8},{12,... | collective-permute-start | bytes 4718600 | tf_op jit(solution)/shard_map/ppermute | solution.py:632
  168.3 88.3 %reduce-scatter.12.cloned.1.call-start = ((), (), s32[]{:S(2)}) async-start(), calls=%async_computation.8 | async-start | bytes 2580480 | tf_op jit(solution)/shard_map/reduce_scatter | solution.py:734
  191.6 34.9 %collective-permute-start.22 = (bf16[2048,384]{1,0:T(8,128)(2,1)}, bf16[2048,384]{1,0:T(8,128)(2,1)S(1)}, u32[]{:S(2)}, u32[]{:S(2)}) collective-permute-start(bf16[2048,384]{1,0:T(8,128)(2,1)} %copy-done.9), channel_id=1, source_target_pairs={{0,4},{2,6},{4,0},{6,2},{1,5},{3,7},{5,1},{7,3},{8,12},{10,14},{12... | collective-permute-start | bytes 4718600 | tf_op jit(solution)/shard_map/ppermute | solution.py:632
  193.0 34.5 %collective-permute-start.23 = (bf16[2048,384]{1,0:T(8,128)(2,1)}, bf16[2048,384]{1,0:T(8,128)(2,1)S(1)}, u32[]{:S(2)}, u32[]{:S(2)}) collective-permute-start(bf16[2048,384]{1,0:T(8,128)(2,1)} %copy-done.10), channel_id=1, source_target_pairs={{0,2},{2,0},{4,6},{6,4},{1,3},{3,1},{5,7},{7,5},{8,10},{10,8},{12,... | collective-permute-start | bytes 4718600 | tf_op jit(solution)/shard_map/ppermute | solution.py:632
  204.9 96.6 %reduce-scatter.14.cloned.1.call-start = ((), (), s32[]{:S(2)}) async-start(), calls=%async_computation.9 | async-start | bytes 2580480 | tf_op jit(solution)/shard_map/reduce_scatter | solution.py:734
  243.6 13.0 %collective-permute-start.24 = (bf16[256,5376]{1,0:T(8,128)(2,1)}, bf16[256,5376]{1,0:T(8,128)(2,1)}, u32[]{:S(2)}, u32[]{:S(2)}) collective-permute-start(bf16[256,5376]{1,0:T(8,128)(2,1)} %get-tuple-element.175), channel_id=1, source_target_pairs={{0,1},{1,0},{2,3},{3,2},{4,5},{5,4},{6,7},{7,6},{8,9},{9,8},{10,11... | collective-permute-start | bytes 8257544 | tf_op jit(solution)/shard_map/ppermute | solution.py:632
  (26 other events, 128.6 us)
Sparse Core Ops, SparseCore 0:
  94.9 22.3 reduce-scatter.5
  130.4 32.4 reduce-scatter.7
  168.4 43.4 reduce-scatter.9
  214.2 42.3 reduce-scatter.11
  258.8 42.6 reduce-scatter.13

commit v3 on v2

--- a/solution.py
+++ b/solution.py
@@ -728,7 +728,10 @@
     first, second, grad_came, input_packed = barrier((first, second, grad_came, input_packed))
 
     input_came = spread(input_packed)
-    grads = joined(grad_own, grad_came)
+    grads = [grad_own, grad_came[0], swap(grad_came[0], "tensor", 1)]
+    grads += [grad_came[1], swap(grad_came[1], "tensor", 1)]
+    grads[2], held = barrier((grads[2], grad_came[2]))
+    grads += [held, swap(held, "tensor", 1)]
     edge = wide + narrow
     def summed(term):
         return lax.psum_scatter(term, "dp", scatter_dimension=0, tiled=True)

time: 311 us -> 312 us (level)
  transfers between devices with their start and end apart: 30 -> 30, of which waited for: 17 -> 18; matrix products, arithmetic and copies ran while one was open for 7% -> 7% of each run, Pallas kernels for 38% -> 38%
where the time goes in v3:
time: 312 us
  waiting for transfers between devices  127 us (41%)
  Pallas kernels  123 us (39%)
  starting transfers between devices  22.5 us (7%)
  between operations  14.1 us (5%)
  other arithmetic  10.6 us (3%)
  matrix products  10.2 us (3%)
  local copies, waits for them, and re-layouts  3.47 us (1%)
    ppermute x25, waiting for transfers between devices, swap(): return lax.ppermute(x, axis, [(i, i ^ by) for i in range(count)])  88.9 us
    pallas_call x5, Pallas kernels, weight_terms(): pl.pallas_call(functools.partial(weight_terms_kernel, blocks, jobs), out_...  49.6 us
    reduce_scatter x5, waiting for transfers between devices, summed(): return lax.psum_scatter(term, 'dp', scatter_dimension=0, tiled=True)  38.3 us
    ppermute x25, starting transfers between devices, swap(): return lax.ppermute(x, axis, [(i, i ^ by) for i in range(count)])  22.3 us
    pallas_call x1, Pallas kernels, attention(): pl.pallas_call(functools.partial(attention_kernel, blocks, count, heads,...  20.7 us
    pallas_call x1, Pallas kernels, input_first(): pl.pallas_call(functools.partial(input_first_kernel, blocks, wide, narrow...  20.1 us
    pallas_call x1, Pallas kernels, input_last(): pl.pallas_call(functools.partial(input_last_kernel, wide), out_shape=(jax...  14.9 us
    pallas_call x2, Pallas kernels, pack_rows(): pl.pallas_call(functools.partial(pack_rows_kernel, blocks, replicas, rows...  10.2 us
  transfers between devices with their start and end apart: 30, of which 18 were waited for; matrix products, arithmetic and copies ran while one was open for 7% of the time, Pallas kernels for 38%

profile of v3, /device:TPU:0, one launch (start us, length us, event | category | flops | bytes accessed | tf_op | source)
XLA Modules:
  0.0 311.7 jit_solution(18214605431538030575)
XLA Ops:
  7.9 3.2 %pack_heads.1 = (bf16[528,512]{1,0:T(8,128)(2,1)}, bf16[528,512]{1,0:T(8,128)(2,1)}, bf16[528,512]{1,0:T(8,128)(2,1)}, bf16[528,512]{1,0:T(8,128)(2,1)}) custom-call(s32[2]{0:T(128)} %pad_add_fusion.1.at_ref.refs_0_, bf16[512,1024]{1,0:T(8,128)(2,1)} %q_ref.1, bf16[512,512]{1,0:T(8,128)(2,1)} %k_ref.1, bf16[512,512]{1,0:T(8,128)(2,1)} %v_ref.1, ...), custom_call_target="tpu_custom_call" | custom-call | bytes 4194304 | tf_op jit(solution)/shard_map/pack_heads/pallas_call | solution.py:228
  11.1 2.9 collective-permute-start
  15.5 10.2 %convolution_convert_fusion = bf16[512,1024]{1,0:T(8,128)(2,1)S(1)} fusion(bf16[512,5376]{1,0:T(8,128)(2,1)} %x_ref.2, bf16[5376,1024]{1,0:T(8,128)(2,1)} %param.19), kind=kOutput, calls=%fused_computation.3 | convolution fusion | flops 5637668864 | bytes 17563648 | tf_op jit(solution)/shard_map/dot_general | solution.py:697
  25.9 4.6 %pack_rows.2 = (bf16[1344,512]{1,0:T(8,128)(2,1)S(1)}, bf16[1344,256]{1,0:T(8,128)(2,1)S(1)}, bf16[1344,256]{1,0:T(8,128)(2,1)S(1)}, bf16[1344,256]{1,0:T(8,128)(2,1)S(1)}) custom-call(s32[2]{0:T(128)S(1)} %copy-done.4, bf16[512,5376]{1,0:T(8,128)(2,1)} %x_ref.2), custom_call_target="tpu_custom_call" | custom-call | bytes 16515072 | tf_op jit(solution)/shard_map/pack_rows/pallas_call | solution.py:269
  31.6 5.6 %pack_rows.3 = (bf16[1344,512]{1,0:T(8,128)(2,1)S(1)}, bf16[1344,256]{1,0:T(8,128)(2,1)}, bf16[1344,256]{1,0:T(8,128)(2,1)S(1)}, bf16[1344,256]{1,0:T(8,128)(2,1)S(1)}) custom-call(s32[2]{0:T(128)S(1)} %copy-done.4, bf16[512,5376]{1,0:T(8,128)(2,1)} %x_ref.3), custom_call_target="tpu_custom_call" | custom-call | bytes 16515072 | tf_op jit(solution)/shard_map/pack_rows/pallas_call | solution.py:269
  37.3 2.2 collective-permute-done.1.refs_3_
  45.2 3.7 %multiply_sine_fusion = (f32[2048,64]{1,0:T(8,128)S(1)}, f32[2048,64]{1,0:T(8,128)S(1)}, f32[2048,64]{1,0:T(8,128)S(1)}) fusion(f32[64]{0:T(128)S(1)} %multiply_power_fusion, f32[2048]{0:T(1024)S(1)} %add_convert_fusion.1), kind=kLoop, calls=%fused_computation.1 | loop fusion | flops 262144 | bytes 1581312 | tf_op jit(solution)/shard_map/sin | solution.py:641
  51.1 3.8 %collective-permute-done.4.refs_7_ = bf16[512,256]{1,0:T(8,128)(2,1)S(1)} collective-permute-done((bf16[512,256]{1,0:T(8,128)(2,1)S(1)}, bf16[512,256]{1,0:T(8,128)(2,1)S(1)}, u32[]{:S(2)}, u32[]{:S(2)}) %collective-permute-start.4) | collective-permute-done | bytes 262176 | tf_op jit(solution)/shard_map/ppermute | solution.py:632
  55.4 20.7 %attention_backward.1 = (bf16[2048,384]{1,0:T(8,128)(2,1)}, bf16[2048,384]{1,0:T(8,128)(2,1)}) custom-call(s32[2]{0:T(128)S(1)} %copy-done.4, bf16[528,512]{1,0:T(8,128)(2,1)S(1)} %copy-done.8, bf16[528,512]{1,0:T(8,128)(2,1)S(1)} %collective-permute-done.refs_2_, bf16[528,512]{1,0:T(8,128)(2,1)S(1)} %collective-permute-done.1.refs_3_, ...), custom_call_target="tpu_custom_call" | custom-call | flops 6710886400 | bytes 6291456 | tf_op jit(solution)/shard_map/attention_backward/pallas_call | solution.py:384
  76.1 6.7 %collective-permute-done.7.refs_3_ = bf16[1344,256]{1,0:T(8,128)(2,1)S(1)} collective-permute-done((bf16[1344,256]{1,0:T(8,128)(2,1)S(1)}, bf16[1344,256]{1,0:T(8,128)(2,1)S(1)}, u32[]{:S(2)}, u32[]{:S(2)}) %collective-permute-start.7) | collective-permute-done | bytes 688160 | tf_op jit(solution)/shard_map/ppermute | solution.py:632
  89.8 6.7 %weight_terms.5 = bf16[1344,256]{1,0:T(8,128)(2,1)} custom-call(s32[2]{0:T(128)} %pad_add_fusion.1.at_ref.refs_0_, bf16[1344,512]{1,0:T(8,128)(2,1)} %copy-done.6, bf16[1344,256]{1,0:T(8,128)(2,1)} %copy-done.14, bf16[1344,256]{1,0:T(8,128)(2,1)} %copy-done.17, bf16[1344,256]{1,0:T(8,128)(2,1)} %copy-done.15, bf16[1344,256]{1,0:T(8,128)(2,1)} %copy-done.18, ...), custom_call_target="tpu_custom_call" | custom-call | flops 8455716864 | bytes 7241728 | tf_op jit(solution)/shard_map/weight_terms/pallas_call | solution.py:446
  96.6 7.2 %collective-permute-done.12.refs_1_.refs_8_ = bf16[1344,256]{1,0:T(8,128)(2,1)} collective-permute-done((bf16[1344,256]{1,0:T(8,128)(2,1)}, bf16[1344,256]{1,0:T(8,128)(2,1)}, u32[]{:S(2)}, u32[]{:S(2)}) %collective-permute-start.12) | collective-permute-done | bytes 688160 | tf_op jit(solution)/shard_map/ppermute | solution.py:632
  103.9 14.2 %collective-permute-done.14.refs_5_.refs_12_ = bf16[1344,256]{1,0:T(8,128)(2,1)} collective-permute-done((bf16[1344,256]{1,0:T(8,128)(2,1)S(1)}, bf16[1344,256]{1,0:T(8,128)(2,1)}, u32[]{:S(2)}, u32[]{:S(2)}) %collective-permute-start.14) | collective-permute-done | bytes 688160 | tf_op jit(solution)/shard_map/ppermute | solution.py:632
  122.5 9.3 %weight_terms.6 = bf16[1344,512]{1,0:T(8,128)(2,1)} custom-call(s32[2]{0:T(128)} %pad_add_fusion.1.at_ref.refs_0_, bf16[1344,512]{1,0:T(8,128)(2,1)} %copy-done.7, bf16[1344,256]{1,0:T(8,128)(2,1)} %collective-permute-done.12.refs_1_.refs_8_, bf16[1344,256]{1,0:T(8,128)(2,1)} %collective-permute-done.15.refs_2_.refs_9_, ...), custom_call_target="tpu_custom_call" | custom-call | flops 16911433728 | bytes 8978432 | tf_op jit(solution)/shard_map/weight_terms/pallas_call | solution.py:446
  131.9 23.7 %collective-permute-done.18.refs_14_.refs_1_ = bf16[2048,384]{1,0:T(8,128)(2,1)S(1)} collective-permute-done((bf16[2048,384]{1,0:T(8,128)(2,1)}, bf16[2048,384]{1,0:T(8,128)(2,1)S(1)}, u32[]{:S(2)}, u32[]{:S(2)}) %collective-permute-start.18) | collective-permute-done | bytes 1572896 | tf_op jit(solution)/shard_map/ppermute | solution.py:632
  158.7 11.2 %weight_terms.7 = bf16[1344,768]{1,0:T(8,128)(2,1)} custom-call(s32[2]{0:T(128)} %pad_add_fusion.1.at_ref.refs_0_, bf16[1344,512]{1,0:T(8,128)(2,1)} %copy-done.6, bf16[1344,256]{1,0:T(8,128)(2,1)} %copy-done.14, bf16[1344,256]{1,0:T(8,128)(2,1)} %copy-done.17, bf16[1344,256]{1,0:T(8,128)(2,1)} %copy-done.15, bf16[1344,256]{1,0:T(8,128)(2,1)} %copy-done.18, ...), custom_call_target="tpu_custom_call" | custom-call | flops 84557168640 | bytes 16220160 | tf_op jit(solution)/shard_map/weight_terms/pallas_call | solution.py:446
  170.0 22.9 %collective-permute-done.20.refs_14_.refs_2_ = bf16[2048,384]{1,0:T(8,128)(2,1)} collective-permute-done((bf16[2048,384]{1,0:T(8,128)(2,1)}, bf16[2048,384]{1,0:T(8,128)(2,1)}, u32[]{:S(2)}, u32[]{:S(2)}) %collective-permute-start.20) | collective-permute-done | bytes 1572896 | tf_op jit(solution)/shard_map/ppermute | solution.py:632
  195.3 11.2 %weight_terms.8 = bf16[1344,768]{1,0:T(8,128)(2,1)} custom-call(s32[2]{0:T(128)} %pad_add_fusion.1.at_ref.refs_0_, bf16[1344,512]{1,0:T(8,128)(2,1)} %copy-done.6, bf16[1344,256]{1,0:T(8,128)(2,1)} %copy-done.14, bf16[1344,256]{1,0:T(8,128)(2,1)} %copy-done.17, bf16[1344,256]{1,0:T(8,128)(2,1)} %copy-done.15, bf16[1344,256]{1,0:T(8,128)(2,1)} %copy-done.18, ...), custom_call_target="tpu_custom_call" | custom-call | flops 84557168640 | bytes 16220160 | tf_op jit(solution)/shard_map/weight_terms/pallas_call | solution.py:446
  206.6 20.1 %input_first.1.part_ref = f32[512,5376]{1,0:T(8,128)} custom-call(s32[2]{0:T(128)} %pad_add_fusion.1.at_ref.refs_0_, bf16[2048,384]{1,0:T(8,128)(2,1)} %get-tuple-element.167.refs_7_.refs_0_, bf16[2048,384]{1,0:T(8,128)(2,1)} %copy-done.9, bf16[2048,384]{1,0:T(8,128)(2,1)} %collective-permute-done.20.refs_14_.refs_2_, ...), custom_call_target="tpu_custom_call" | custom-call | flops 5637144576 | tf_op jit(solution)/shard_map/input_first/pallas_call | solution.py:571
  230.4 14.9 %input_last.1 = (f32[256,5376]{1,0:T(8,128)}, bf16[256,5376]{1,0:T(8,128)(2,1)}) custom-call(s32[2]{0:T(128)} %pad_add_fusion.1.at_ref.refs_0_, bf16[2048,384]{1,0:T(8,128)(2,1)} %copy-done.12, bf16[2048,384]{1,0:T(8,128)(2,1)} %copy-done.13, bf16[5376,1024]{1,0:T(8,128)(2,1)} %wq_ref.1, bf16[5376,512]{1,0:T(8,128)(2,1)} %wk_ref.1, ...), custom_call_target="tpu_custom_call" | custom-call | flops 112742891520 | tf_op jit(solution)/shard_map/input_last/pallas_call | solution.py:608
  245.2 11.2 %weight_terms.9 = bf16[1344,768]{1,0:T(8,128)(2,1)} custom-call(s32[2]{0:T(128)} %pad_add_fusion.1.at_ref.refs_0_, bf16[1344,512]{1,0:T(8,128)(2,1)} %copy-done.6, bf16[1344,256]{1,0:T(8,128)(2,1)} %copy-done.14, bf16[1344,256]{1,0:T(8,128)(2,1)} %copy-done.17, bf16[1344,256]{1,0:T(8,128)(2,1)} %copy-done.15, bf16[1344,256]{1,0:T(8,128)(2,1)} %copy-done.18, ...), custom_call_target="tpu_custom_call" | custom-call | flops 84557168640 | bytes 16220160 | tf_op jit(solution)/shard_map/weight_terms/pallas_call | solution.py:446
  258.3 5.5 %add_convert_fusion = bf16[256,5376]{1,0:T(8,128)(2,1)} fusion(f32[256,5376]{1,0:T(8,128)} %get-tuple-element.180, bf16[256,5376]{1,0:T(8,128)(2,1)} %collective-permute-done.24), kind=kLoop, calls=%fused_computation | loop fusion | flops 4128768 | bytes 11010048 | tf_op jit(solution)/shard_map/convert_element_type | solution.py:786
  263.8 2.7 assemble.1
  266.6 36.4 %reduce-scatter.14.cloned.1.call-done.part_ref = bf16[336,768]{1,0:T(8,128)(2,1)} async-done(((bf16[1344,768]{1,0:T(8,128)(2,1)}), bf16[336,768]{1,0:T(8,128)(2,1)}) %reduce-scatter.14.cloned.1.call-update) | async-done | bytes 516112 | tf_op jit(solution)/shard_map/reduce_scatter | solution.py:737
  (110 shorter events, 36.7 us)
Async XLA Ops:
  7.2 115.4 %reduce-scatter.6.cloned.1.call-start = ((), (), s32[]{:S(2)}) async-start(), calls=%async_computation.5 | async-start | bytes 860160 | tf_op jit(solution)/shard_map/reduce_scatter | solution.py:737
  11.1 26.3 %collective-permute-start = (bf16[528,512]{1,0:T(8,128)(2,1)}, bf16[528,512]{1,0:T(8,128)(2,1)S(1)}, u32[]{:S(2)}, u32[]{:S(2)}) collective-permute-start(bf16[528,512]{1,0:T(8,128)(2,1)} %get-tuple-element.109), channel_id=1, source_target_pairs={{0,2},{2,0},{4,6},{6,4},{1,3},{3,1},{5,7},{7,5},{8,10},{10,8},{12,... | collective-permute-start | bytes 1622024 | tf_op jit(solution)/shard_map/ppermute | solution.py:632
  14.0 25.5 %collective-permute-start.1 = (bf16[528,512]{1,0:T(8,128)(2,1)}, bf16[528,512]{1,0:T(8,128)(2,1)S(1)}, u32[]{:S(2)}, u32[]{:S(2)}) collective-permute-start(bf16[528,512]{1,0:T(8,128)(2,1)} %get-tuple-element.110), channel_id=1, source_target_pairs={{0,4},{2,6},{4,0},{6,2},{1,5},{3,7},{5,1},{7,3},{8,12},{10,14},{12... | collective-permute-start | bytes 1622024 | tf_op jit(solution)/shard_map/ppermute | solution.py:632
  15.5 24.0 %collective-permute-start.2 = (bf16[528,512]{1,0:T(8,128)(2,1)}, bf16[528,512]{1,0:T(8,128)(2,1)S(1)}, u32[]{:S(2)}, u32[]{:S(2)}) collective-permute-start(bf16[528,512]{1,0:T(8,128)(2,1)} %get-tuple-element.111), channel_id=1, source_target_pairs={{0,6},{2,4},{4,2},{6,0},{1,7},{3,5},{5,3},{7,1},{8,14},{10,12},{12... | collective-permute-start | bytes 1622024 | tf_op jit(solution)/shard_map/ppermute | solution.py:632
  39.5 10.1 %collective-permute-start.3 = (bf16[512,256]{1,0:T(8,128)(2,1)S(1)}, bf16[512,256]{1,0:T(8,128)(2,1)S(1)}, u32[]{:S(2)}, u32[]{:S(2)}) collective-permute-start(bf16[512,256]{1,0:T(8,128)(2,1)S(1)} %get-tuple-element.131), channel_id=1, source_target_pairs={{0,2},{2,0},{4,6},{6,4},{1,3},{3,1},{5,7},{7,5},{8,10},{10,8},{12,... | collective-permute-start | bytes 786440 | tf_op jit(solution)/shard_map/ppermute | solution.py:632
  40.8 14.1 %collective-permute-start.4 = (bf16[512,256]{1,0:T(8,128)(2,1)S(1)}, bf16[512,256]{1,0:T(8,128)(2,1)S(1)}, u32[]{:S(2)}, u32[]{:S(2)}) collective-permute-start(bf16[512,256]{1,0:T(8,128)(2,1)S(1)} %get-tuple-element.132), channel_id=1, source_target_pairs={{0,4},{2,6},{4,0},{6,2},{1,5},{3,7},{5,1},{7,3},{8,12},{10,14},{12... | collective-permute-start | bytes 786440 | tf_op jit(solution)/shard_map/ppermute | solution.py:632
  41.7 13.8 %collective-permute-start.5 = (bf16[512,256]{1,0:T(8,128)(2,1)S(1)}, bf16[512,256]{1,0:T(8,128)(2,1)S(1)}, u32[]{:S(2)}, u32[]{:S(2)}) collective-permute-start(bf16[512,256]{1,0:T(8,128)(2,1)S(1)} %get-tuple-element.133), channel_id=1, source_target_pairs={{0,6},{2,4},{4,2},{6,0},{1,7},{3,5},{5,3},{7,1},{8,14},{10,12},{12... | collective-permute-start | bytes 786440 | tf_op jit(solution)/shard_map/ppermute | solution.py:632
  43.1 33.0 %collective-permute-start.6 = (bf16[1344,256]{1,0:T(8,128)(2,1)S(1)}, bf16[1344,256]{1,0:T(8,128)(2,1)S(1)}, u32[]{:S(2)}, u32[]{:S(2)}) collective-permute-start(bf16[1344,256]{1,0:T(8,128)(2,1)S(1)} %get-tuple-element.136), channel_id=1, source_target_pairs={{0,2},{2,0},{4,6},{6,4},{1,3},{3,1},{5,7},{7,5},{8,10},{10,8},{12,... | collective-permute-start | bytes 2064392 | tf_op jit(solution)/shard_map/ppermute | solution.py:632
  44.3 38.5 %collective-permute-start.7 = (bf16[1344,256]{1,0:T(8,128)(2,1)S(1)}, bf16[1344,256]{1,0:T(8,128)(2,1)S(1)}, u32[]{:S(2)}, u32[]{:S(2)}) collective-permute-start(bf16[1344,256]{1,0:T(8,128)(2,1)S(1)} %get-tuple-element.137), channel_id=1, source_target_pairs={{0,4},{2,6},{4,0},{6,2},{1,5},{3,7},{5,1},{7,3},{8,12},{10,14},{12... | collective-permute-start | bytes 2064392 | tf_op jit(solution)/shard_map/ppermute | solution.py:632
  49.6 33.2 %collective-permute-start.8 = (bf16[1344,256]{1,0:T(8,128)(2,1)S(1)}, bf16[1344,256]{1,0:T(8,128)(2,1)S(1)}, u32[]{:S(2)}, u32[]{:S(2)}) collective-permute-start(bf16[1344,256]{1,0:T(8,128)(2,1)S(1)} %get-tuple-element.138), channel_id=1, source_target_pairs={{0,6},{2,4},{4,2},{6,0},{1,7},{3,5},{5,3},{7,1},{8,14},{10,12},{12... | collective-permute-start | bytes 2064392 | tf_op jit(solution)/shard_map/ppermute | solution.py:632
  85.2 18.6 %collective-permute-start.12 = (bf16[1344,256]{1,0:T(8,128)(2,1)}, bf16[1344,256]{1,0:T(8,128)(2,1)}, u32[]{:S(2)}, u32[]{:S(2)}) collective-permute-start(bf16[1344,256]{1,0:T(8,128)(2,1)} %get-tuple-element.149), channel_id=1, source_target_pairs={{0,2},{2,0},{4,6},{6,4},{1,3},{3,1},{5,7},{7,5},{8,10},{10,8},{12,... | collective-permute-start | bytes 2064392 | tf_op jit(solution)/shard_map/ppermute | solution.py:632
  85.8 18.1 %collective-permute-start.13 = (bf16[1344,256]{1,0:T(8,128)(2,1)S(1)}, bf16[1344,256]{1,0:T(8,128)(2,1)}, u32[]{:S(2)}, u32[]{:S(2)}) collective-permute-start(bf16[1344,256]{1,0:T(8,128)(2,1)S(1)} %get-tuple-element.150), channel_id=1, source_target_pairs={{0,4},{2,6},{4,0},{6,2},{1,5},{3,7},{5,1},{7,3},{8,12},{10,14},{12... | collective-permute-start | bytes 2064392 | tf_op jit(solution)/shard_map/ppermute | solution.py:632
  86.9 31.1 %collective-permute-start.14 = (bf16[1344,256]{1,0:T(8,128)(2,1)S(1)}, bf16[1344,256]{1,0:T(8,128)(2,1)}, u32[]{:S(2)}, u32[]{:S(2)}) collective-permute-start(bf16[1344,256]{1,0:T(8,128)(2,1)S(1)} %get-tuple-element.151), channel_id=1, source_target_pairs={{0,6},{2,4},{4,2},{6,0},{1,7},{3,5},{5,3},{7,1},{8,14},{10,12},{12... | collective-permute-start | bytes 2064392 | tf_op jit(solution)/shard_map/ppermute | solution.py:632
  96.5 130.2 %reduce-scatter.8.cloned.1.call-start = ((), (), s32[]{:S(2)}) async-start(), calls=%async_computation.6 | async-start | bytes 1720320 | tf_op jit(solution)/shard_map/reduce_scatter | solution.py:737
  118.6 37.0 %collective-permute-start.18 = (bf16[2048,384]{1,0:T(8,128)(2,1)}, bf16[2048,384]{1,0:T(8,128)(2,1)S(1)}, u32[]{:S(2)}, u32[]{:S(2)}) collective-permute-start(bf16[2048,384]{1,0:T(8,128)(2,1)} %get-tuple-element.167.refs_7_.refs_0_), channel_id=1, source_target_pairs={{0,2},{2,0},{4,6},{6,4},{1,3},{3,1},{5,7},{7,5},{8,10},{10,8},{12,... | collective-permute-start | bytes 4718600 | tf_op jit(solution)/shard_map/ppermute | solution.py:632
  120.0 36.7 %collective-permute-start.19 = (bf16[2048,384]{1,0:T(8,128)(2,1)}, bf16[2048,384]{1,0:T(8,128)(2,1)S(1)}, u32[]{:S(2)}, u32[]{:S(2)}) collective-permute-start(bf16[2048,384]{1,0:T(8,128)(2,1)} %get-tuple-element.168.refs_8_.refs_3_), channel_id=1, source_target_pairs={{0,4},{2,6},{4,0},{6,2},{1,5},{3,7},{5,1},{7,3},{8,12},{10,14},{12... | collective-permute-start | bytes 4718600 | tf_op jit(solution)/shard_map/ppermute | solution.py:632
  131.9 124.6 %reduce-scatter.10.cloned.1.call-start = ((), (), s32[]{:S(2)}) async-start(), calls=%async_computation.7 | async-start | bytes 2580480 | tf_op jit(solution)/shard_map/reduce_scatter | solution.py:737
  156.8 36.1 %collective-permute-start.20 = (bf16[2048,384]{1,0:T(8,128)(2,1)}, bf16[2048,384]{1,0:T(8,128)(2,1)}, u32[]{:S(2)}, u32[]{:S(2)}) collective-permute-start(bf16[2048,384]{1,0:T(8,128)(2,1)} %get-tuple-element.167.refs_7_.refs_0_), channel_id=1, source_target_pairs={{0,4},{2,6},{4,0},{6,2},{1,5},{3,7},{5,1},{7,3},{8,12},{10,14},{12... | collective-permute-start | bytes 4718600 | tf_op jit(solution)/shard_map/ppermute | solution.py:632
  157.3 35.9 %collective-permute-start.21 = (bf16[2048,384]{1,0:T(8,128)(2,1)}, bf16[2048,384]{1,0:T(8,128)(2,1)}, u32[]{:S(2)}, u32[]{:S(2)}) collective-permute-start(bf16[2048,384]{1,0:T(8,128)(2,1)} %get-tuple-element.168.refs_8_.refs_3_), channel_id=1, source_target_pairs={{0,2},{2,0},{4,6},{6,4},{1,3},{3,1},{5,7},{7,5},{8,10},{10,8},{12,... | collective-permute-start | bytes 4718600 | tf_op jit(solution)/shard_map/ppermute | solution.py:632
  169.9 88.4 %reduce-scatter.12.cloned.1.call-start = ((), (), s32[]{:S(2)}) async-start(), calls=%async_computation.8 | async-start | bytes 2580480 | tf_op jit(solution)/shard_map/reduce_scatter | solution.py:737
  193.2 34.9 %collective-permute-start.22 = (bf16[2048,384]{1,0:T(8,128)(2,1)}, bf16[2048,384]{1,0:T(8,128)(2,1)S(1)}, u32[]{:S(2)}, u32[]{:S(2)}) collective-permute-start(bf16[2048,384]{1,0:T(8,128)(2,1)} %copy-done.9), channel_id=1, source_target_pairs={{0,4},{2,6},{4,0},{6,2},{1,5},{3,7},{5,1},{7,3},{8,12},{10,14},{12... | collective-permute-start | bytes 4718600 | tf_op jit(solution)/shard_map/ppermute | solution.py:632
  194.6 34.5 %collective-permute-start.23 = (bf16[2048,384]{1,0:T(8,128)(2,1)}, bf16[2048,384]{1,0:T(8,128)(2,1)S(1)}, u32[]{:S(2)}, u32[]{:S(2)}) collective-permute-start(bf16[2048,384]{1,0:T(8,128)(2,1)} %copy-done.10), channel_id=1, source_target_pairs={{0,2},{2,0},{4,6},{6,4},{1,3},{3,1},{5,7},{7,5},{8,10},{10,8},{12,... | collective-permute-start | bytes 4718600 | tf_op jit(solution)/shard_map/ppermute | solution.py:632
  206.5 96.5 %reduce-scatter.14.cloned.1.call-start = ((), (), s32[]{:S(2)}) async-start(), calls=%async_computation.9 | async-start | bytes 2580480 | tf_op jit(solution)/shard_map/reduce_scatter | solution.py:737
  245.2 13.1 %collective-permute-start.24 = (bf16[256,5376]{1,0:T(8,128)(2,1)}, bf16[256,5376]{1,0:T(8,128)(2,1)}, u32[]{:S(2)}, u32[]{:S(2)}) collective-permute-start(bf16[256,5376]{1,0:T(8,128)(2,1)} %get-tuple-element.179), channel_id=1, source_target_pairs={{0,1},{1,0},{2,3},{3,2},{4,5},{5,4},{6,7},{7,6},{8,9},{9,8},{10,11... | collective-permute-start | bytes 8257544 | tf_op jit(solution)/shard_map/ppermute | solution.py:632
  (26 other events, 137.7 us)
Sparse Core Ops, SparseCore 0:
  96.6 22.4 reduce-scatter.5
  132.0 32.4 reduce-scatter.7
  170.0 43.4 reduce-scatter.9
  215.9 42.4 reduce-scatter.11
  260.5 42.4 reduce-scatter.13
